TPU v7x, 512 devices: a whole 4x8x8 slice. The times are simulated.
512 devices in a mesh: leaf: 128 (over y, z, core), rhs: 4 (over x).
Axes of the slice: x: 4, y: 8, z: 8, core: 2. Of those that a mesh axis runs over, the one named last changes fastest.
Arguments:
- rhs_block: bfloat16 [128, 1048576], P('rhs', 'leaf'), may hold values from -6 to 6
- points: float32 [32, 1048576], P(None, 'leaf'), may hold values from -1.5 to 1.5
- basis: bfloat16 [2048, 512, 128], P('leaf'), may hold values from -0.25 to 0.25
- skeleton_leaf: int32 [2048, 128], P('leaf'), may hold values from 0 to 511, as said below
- skeleton_lower: int32 [512, 128], P('leaf'), may hold values from 0 to 511, as said below
- skeleton_upper: int32 [128, 128], P('leaf'), may hold values from 0 to 511, as said below
- skeleton_top: int32 [32, 128], replicated, may hold values from 0 to 511, as said below
- transfer_leaf: bfloat16 [2048, 128, 128], P('leaf'), may hold values from -0.25 to 0.25
- transfer_lower: bfloat16 [512, 128, 128], P('leaf'), may hold values from -0.25 to 0.25
- transfer_upper: bfloat16 [128, 128, 128], P('leaf'), may hold values from -0.25 to 0.25
Outputs:
- product: bfloat16 [128, 1048576], P('rhs', 'leaf')
Inputs may be any that keep to these rules, and one draw needn't show every extreme that they name: `skeleton_leaf`: the 128 entries of a row are distinct rows of the leaf. `skeleton_lower`: the 128 entries of a row are distinct. `skeleton_upper`: the 128 entries of a row are distinct. `skeleton_top`: the 128 entries of a row are distinct.
All inputs are finite; a program needn't handle non-finite values.
Results may differ from a plain program's by a relative error of at most 0.0038.
The roundings to bfloat16 on the way count: a program that leaves them out, or rounds other values in their place, can miss the bound.
Values may be sent and summed in bfloat16 or wider, within the bound.
No kernel may reach another device: no remote copies, remote signals or barrier semaphores. Data moves between devices by JAX's collectives and lax.ppermute only.
A program may use at most 64 MiB of HBM per device.

v0:
```python
import jax
import jax.numpy as jnp
from jax import lax
from jax.sharding import PartitionSpec as P

RIDGE = 1.0
HIGH = lax.Precision.HIGHEST


def from_partner(shard, axis, apart):
    return lax.ppermute(shard, axis, [(i, i ^ 1 << apart) for i in range(lax.axis_size(axis))])


def kernel_block(left, right):
    left_sq = jnp.sum(left * left, axis=0)
    right_sq = jnp.sum(right * right, axis=0)
    cross = jnp.dot(left.T, right, precision=HIGH, preferred_element_type=jnp.float32)
    return jnp.exp(-(left_sq[:, None] + right_sq[None, :] - 2.0 * cross))


def sibling_terms(coeffs, places):
    count = coeffs.shape[0] // 4
    grouped = (
        coeffs.reshape((count, 4) + coeffs.shape[1:]),
        places.reshape((count, 4) + places.shape[1:]),
    )

    def per_group(pair):
        group_coeffs, group_places = pair
        result = []
        for target in range(4):
            total = jnp.zeros(group_coeffs.shape[1:], jnp.float32)
            for source in range(4):
                if source != target:
                    total = total + jnp.dot(
                        group_coeffs[source],
                        kernel_block(group_places[source], group_places[target]),
                        precision=HIGH,
                        preferred_element_type=jnp.float32,
                    )
            result.append(total)
        return jnp.stack(result)

    return lax.map(per_group, grouped).reshape(coeffs.shape)


def parent_places(places, index):
    count = places.shape[0] // 4
    dims_here, rank_here = (places.shape[1], places.shape[2])
    candidates = (
        places.reshape(count, 4, dims_here, rank_here)
        .transpose(0, 2, 1, 3)
        .reshape(count, dims_here, 4 * rank_here)
    )
    return jnp.take_along_axis(candidates, index[:, None, :], axis=2)


def lift(coeffs, transfer):
    moved = jnp.einsum("nrk,nkm->nrm", coeffs, transfer.astype(jnp.float32), precision=HIGH)
    count = coeffs.shape[0] // 4
    return moved.reshape((count, 4) + moved.shape[1:]).sum(axis=1)


def descend(parent_terms, transfer, local_terms):
    repeated = jnp.repeat(parent_terms, 4, axis=0)
    return local_terms + jnp.einsum(
        "nrm,nkm->nrk", repeated, transfer.astype(jnp.float32), precision=HIGH
    )


def near_block(place, values):
    squares = jnp.sum(place * place, axis=1)
    cross = jnp.einsum(
        "kdm,kdn->kmn", place, place, precision=HIGH, preferred_element_type=jnp.float32
    )
    block = jnp.exp(-(squares[:, :, None] + squares[:, None, :] - 2.0 * cross)).astype(jnp.bfloat16)
    total = jnp.einsum(
        "kcm,kmn->kcn", values, block, preferred_element_type=jnp.float32
    ) + RIDGE * values.astype(jnp.float32)
    return total.astype(jnp.bfloat16)


def make_fold(each, node, place_top, pieces):
    piece_coeffs, piece_places = pieces
    column = jnp.arange(piece_coeffs.shape[1], dtype=jnp.int32)
    source = column // each
    keep = source // 4 != node
    masked = jnp.where(keep[None, :], piece_coeffs, 0.0)
    return jnp.dot(
        masked,
        kernel_block(piece_places, place_top),
        precision=HIGH,
        preferred_element_type=jnp.float32,
    )


def per_device(
    rhs_block,
    points,
    basis,
    skeleton_leaf,
    skeleton_lower,
    skeleton_upper,
    skeleton_top,
    transfer_leaf,
    transfer_lower,
    transfer_upper,
):
    rows, width = rhs_block.shape
    leaves, leaf, rank = basis.shape
    dims = points.shape[0]
    leaf_points = points.reshape(dims, leaves, leaf).transpose(1, 0, 2)
    leaf_rhs = rhs_block.reshape(rows, leaves, leaf).transpose(1, 0, 2)
    parts = lax.axis_size("rhs")
    share = leaves // parts
    spread = lax.all_to_all(rhs_block, "rhs", split_axis=1, concat_axis=0, tiled=True)
    first = lax.axis_index("rhs") * share
    own_points = lax.dynamic_slice_in_dim(leaf_points, first, share, 0)
    own_rhs = spread.reshape(rows * parts, share, leaf).transpose(1, 0, 2)
    near_own = near_block(own_points, own_rhs)
    near_flat = near_own.transpose(1, 0, 2).reshape(rows * parts, share * leaf)
    returned = lax.all_to_all(near_flat, "rhs", split_axis=0, concat_axis=1, tiled=True)
    near = returned.reshape(rows, leaves, leaf).transpose(1, 0, 2)
    coeff_leaf = jnp.einsum("lcp,lpk->lck", leaf_rhs, basis, preferred_element_type=jnp.float32)
    place_leaf = jnp.take_along_axis(leaf_points, skeleton_leaf[:, None, :], axis=2)
    coeff_lower = lift(coeff_leaf, transfer_leaf)
    place_lower = parent_places(place_leaf, skeleton_lower)
    coeff_upper = lift(coeff_lower, transfer_lower)
    place_upper = parent_places(place_lower, skeleton_upper)
    leaf_terms = sibling_terms(coeff_leaf, place_leaf)
    lower_terms = sibling_terms(coeff_lower, place_lower)
    raised = jnp.dot(
        coeff_upper[0],
        transfer_upper[0].astype(jnp.float32),
        precision=HIGH,
        preferred_element_type=jnp.float32,
    )
    held_coeffs, held_places, held_raised = (coeff_upper, place_upper, raised[None])
    for bit in range(2):
        got_coeffs, got_places, got_raised = from_partner(
            (held_coeffs, held_places, held_raised), "leaf", bit
        )
        held_coeffs = jnp.concatenate([held_coeffs, got_coeffs], 0)
        held_places = jnp.concatenate([held_places, got_places], 0)
        held_raised = jnp.concatenate([held_raised, got_raised], 0)
    upper_terms = jnp.zeros((rows, rank), jnp.float32)
    for offset in range(1, 4):
        upper_terms = upper_terms + jnp.dot(
            held_coeffs[offset],
            kernel_block(held_places[offset], place_upper[0]),
            precision=HIGH,
            preferred_element_type=jnp.float32,
        )
    coeff_top = jnp.sum(held_raised, axis=0)
    position = lax.axis_index("leaf")
    in_group = position % 4
    node = position // 4
    candidates = jnp.concatenate(
        [
            lax.dynamic_index_in_dim(held_places, in_group ^ child, 0, keepdims=False)
            for child in range(4)
        ],
        1,
    )
    top_index = lax.dynamic_index_in_dim(skeleton_top, node, 0, keepdims=False)
    place_top = jnp.take(candidates, top_index, axis=1)
    quarter = rank // 4
    offset_cols = in_group * quarter
    send_coeffs = lax.dynamic_slice_in_dim(coeff_top, offset_cols, quarter, 1)
    send_places = lax.dynamic_slice_in_dim(place_top, offset_cols, quarter, 1)
    top_terms = make_fold(
        quarter,
        node,
        place_top,
        (
            lax.all_gather(send_coeffs, "leaf", axis=1, tiled=True),
            lax.all_gather(send_places, "leaf", axis=1, tiled=True),
        ),
    )
    upper_full = (
        upper_terms
        + jnp.dot(
            top_terms,
            transfer_upper[0].astype(jnp.float32).T,
            precision=HIGH,
            preferred_element_type=jnp.float32,
        )
    )[None]
    lower_full = descend(upper_full, transfer_lower, lower_terms)
    leaf_full = descend(lower_full, transfer_leaf, leaf_terms).astype(jnp.bfloat16)
    far = jnp.einsum("lck,lpk->lcp", leaf_full, basis, preferred_element_type=jnp.float32)
    result = (near.astype(jnp.float32) + far).astype(jnp.bfloat16)
    return result.transpose(1, 0, 2).reshape(rows, width)


def solution(mesh):
    return jax.shard_map(
        per_device,
        mesh=mesh,
        in_specs=(
            P("rhs", "leaf"),
            P(None, "leaf"),
            P("leaf", None, None),
            P("leaf", None),
            P("leaf", None),
            P("leaf", None),
            P(),
            P("leaf", None, None),
            P("leaf", None, None),
            P("leaf", None, None),
        ),
        out_specs=P("rhs", "leaf"),
        check_vma=False,
    )
```

profile of v0, /device:TPU:1, one launch (start us, length us, event | category | flops | bytes accessed | tf_op | source)
XLA Modules:
  0.0 281.9 jit_solution(13071368599434812359)
XLA Ops:
  4.9 1.8 copy.69
  6.7 2.6 copy.53
  9.4 30.0 %gather_fusion.2 = f32[2048,32]{1,0:T(8,128)} fusion(f32[16,32,512]{1,2,0:T(8,128)} %bitcast.438, s32[2048]{0:T(1024)S(1)} %fusion.169), kind=kCustom, calls=%fused_computation.2 | custom fusion | bytes 540672 | tf_op jit(solution)/shard_map/jit(take_along_axis)/gather | solution.py:125
  43.6 6.0 %gather_fusion.3 = f32[512,32]{1,0:T(8,128)} fusion(f32[4,32,512]{1,2,0:T(8,128)S(1)} %bitcast.442, s32[512]{0:T(512)S(1)} %fusion.170), kind=kCustom, calls=%fused_computation.3 | custom fusion | bytes 135168 | tf_op jit(solution)/shard_map/jit(take_along_axis)/gather | solution.py:55
  51.6 8.9 %collective-permute-start.1 = (f32[1,32,128]{1,2,0:T(8,128)S(1)}, f32[1,32,128]{1,2,0:T(8,128)}, u32[]{:S(2)}, u32[]{:S(2)}) collective-permute-start(f32[1,32,128]{1,2,0:T(8,128)S(1)} %bitcast_select_fusion), channel_id=1, source_target_pairs={{0,4},{4,0},{8,12},{12,8},{16,20},{20,16},{24,28},{28,24},{32,36},... | collective-permute-start | bytes 49160 | tf_op jit(solution)/shard_map/ppermute | solution.py:11
  63.4 1.9 collective-permute-start
  66.1 2.4 collective-permute-start.4
  69.4 3.8 %all-to-all-start = ((bf16[32,4,2048]{2,0,1:T(8,128)(2,1)}), bf16[32,4,2048]{2,0,1:T(8,128)(2,1)S(1)}, u32[]{:S(2)}, u32[]{:S(2)}) async-start(bf16[32,4,2048]{2,0,1:T(8,128)(2,1)} %bitcast.446), calls=%async_computation | async-start | bytes 1048576 | tf_op jit(solution)/shard_map/all_to_all | solution.py:116
  73.2 1.6 fusion.140
  91.9 25.7 %while.2 = (s32[]{:T(128)}, f32[4,4,32,128]{3,2,1,0:T(8,128)}, f32[4,4,32,128]{3,2,1,0:T(8,128)S(1)}, f32[4,4,32,128]{3,2,1,0:T(8,128)S(1)}, s32[]{:T(128)}, /*index=5*/s32[]{:T(128)}, s32[]{}, s32[]{}, s32[]{}) while((s32[]{:T(128)}, f32[4,4,32,128]{3,2,1,0:T(8,128)}, f32[4,4,32,128]{3,2,1,0:T(8,128)S(1)}, f32[4,4,32,128]{3,2,1,0:T(8,128)S(1)}, ...), condition=%wide.region_6.7_spmd, body=%wide.region_1.6_spmd.sunk | while | flops 151895552 | bytes 2714413 | solution.py:44
  118.9 5.3 %exponential_convert_fusion = bf16[4,512,512]{2,1,0:T(8,128)(2,1)} fusion(f32[4,512]{1,0:T(4,128)S(1)} %multiply_reduce_fusion.5, f32[32,4,512]{2,1,0:T(4,128)S(1)} %constant_dynamic-slice_fusion.1), kind=kOutput, calls=%fused_computation.110 | convolution fusion | flops 407896064 | bytes 2367488 | tf_op jit(solution)/shard_map/kdm,kdn->kmn/dot_general | solution.py:73
  129.8 1.9 collective-permute-start.3
  132.4 3.4 %collective-permute-start.2 = (f32[2,32,128]{2,1,0:T(8,128)S(1)}, f32[2,32,128]{2,1,0:T(8,128)S(1)}, u32[]{:S(2)}, u32[]{:S(2)}) collective-permute-start(f32[2,32,128]{2,1,0:T(8,128)S(1)} %pad_maximum_fusion.2), channel_id=1, source_target_pairs={{0,8},{4,12},{8,0},{12,4},{16,24},{20,28},{24,16},{28,20},{32,40},... | collective-permute-start | bytes 98312 | tf_op jit(solution)/shard_map/ppermute | solution.py:11
  136.5 1.9 collective-permute-start.5
  141.6 54.5 %all_gather.7 = f32[32,4096]{0,1:T(8,128)S(1)} all-gather(f32[32,32]{0,1:T(8,128)S(1)} %dynamic-slice_bitcast_fusion.44), channel_id=1, replica_groups=mesh['leaf'=128,'rhs'=4] {'leaf'}, dimensions={1}, use_global_device_ids=true | all-gather | bytes 528384 | tf_op jit(solution)/shard_map/all_gather | solution.py:177
  198.9 49.7 %all_gather.6 = f32[32,4096]{0,1:T(8,128)S(1)} all-gather(f32[32,32]{0,1:T(8,128)S(1)} %copy.58), channel_id=1, replica_groups=mesh['leaf'=128,'rhs'=4] {'leaf'}, dimensions={1}, use_global_device_ids=true | all-gather | bytes 528384 | tf_op jit(solution)/shard_map/all_gather | solution.py:176
  248.6 2.0 fusion.71
  250.7 4.1 %fusion.72 = f32[32,128]{1,0:T(8,128)S(1)} fusion(f32[4096,128]{1,0:T(8,128)S(1)} %fusion.71, f32[32,4096]{0,1:T(8,128)S(1)} %all_gather.6, pred[4096]{0:T(1024)(128)(4,1)S(1)} %copy-done.29), kind=kOutput, calls=%fused_computation.112 | convolution fusion | flops 201457664 | bytes 2641920 | tf_op jit(solution)/shard_map/dot_general | solution.py:89
  258.5 2.5 fusion.77
  262.7 4.8 %all-to-all-start.1 = ((bf16[4,32,2048]{2,1,0:T(8,128)(2,1)}), bf16[4,32,2048]{2,1,0:T(8,128)(2,1)S(1)}, u32[]{:S(2)}, u32[]{:S(2)}) async-start(bf16[4,32,2048]{2,1,0:T(8,128)(2,1)} %all_to_all.25), calls=%async_computation.1 | async-start | bytes 1048576 | tf_op jit(solution)/shard_map/all_to_all | solution.py:122
  267.9 1.9 fusion.79
  269.7 6.9 %all-to-all-done.1 = bf16[4,32,2048]{2,1,0:T(8,128)(2,1)S(1)} async-done(((bf16[4,32,2048]{2,1,0:T(8,128)(2,1)}), bf16[4,32,2048]{2,1,0:T(8,128)(2,1)S(1)}, u32[]{:S(2)}, u32[]{:S(2)}) %all-to-all-start.1) | async-done | bytes 524320 | tf_op jit(solution)/shard_map/all_to_all | solution.py:122
  277.4 1.5 reshape.381
  278.9 2.1 fusion.78
  (262 shorter events, 78.5 us)
Async XLA Ops:
  0.0 60.6 %copy-start = (bf16[16,512,128]{2,1,0:T(8,128)(2,1)S(1)}, bf16[16,512,128]{2,1,0:T(8,128)(2,1)}, u32[]{:S(2)}) copy-start(bf16[16,512,128]{2,1,0:T(8,128)(2,1)} %param.14) | copy-start | bytes 6291460
  1.6 39.4 %copy-start.27 = (pred[16,128]{1,0:T(8,128)(4,1)}, pred[16,128]{1,0:T(8,128)(4,1)S(1)}, u32[]{:S(2)}) copy-start(pred[16,128]{1,0:T(8,128)(4,1)S(1)} %compare_and_fusion) | copy-start | bytes 6148
  2.9 46.7 %copy-start.31 = (pred[4,128]{1,0:T(4,128)(4,1)}, pred[4,128]{1,0:T(4,128)(4,1)S(1)}, u32[]{:S(2)}) copy-start(pred[4,128]{1,0:T(4,128)(4,1)S(1)} %compare_and_fusion.3) | copy-start | bytes 1540
  3.6 47.9 %copy-start.32 = (pred[128]{0:T(512)(128)(4,1)}, pred[128]{0:T(512)(128)(4,1)S(1)}, u32[]{:S(2)}) copy-start(pred[128]{0:T(512)(128)(4,1)S(1)} %compare_and_fusion.2) | copy-start | bytes 388
  49.7 12.4 %copy-start.6 = (bf16[16,128,128]{2,1,0:T(8,128)(2,1)S(1)}, bf16[16,128,128]{2,1,0:T(8,128)(2,1)}, u32[]{:S(2)}) copy-start(bf16[16,128,128]{2,1,0:T(8,128)(2,1)} %param.19) | copy-start | bytes 1572868
  50.8 11.7 %copy-start.10 = (bf16[4,128,128]{2,1,0:T(8,128)(2,1)S(1)}, bf16[4,128,128]{2,1,0:T(8,128)(2,1)}, u32[]{:S(2)}) copy-start(bf16[4,128,128]{2,1,0:T(8,128)(2,1)} %param.20) | copy-start | bytes 393220
  50.8 14.4 %copy-start.21 = (bf16[1,128,128]{2,1,0:T(8,128)(2,1)S(1)}, bf16[1,128,128]{2,1,0:T(8,128)(2,1)}, u32[]{:S(2)}) copy-start(bf16[1,128,128]{2,1,0:T(8,128)(2,1)} %param.21) | copy-start | bytes 98308
  51.5 17.9 %copy-start.12 = (f32[128,32]{1,0:T(8,128)}, f32[128,32]{1,0:T(8,128)S(1)}, u32[]{:S(2)}) copy-start(f32[128,32]{1,0:T(8,128)S(1)} %gather_fusion) | copy-start | bytes 49156
  51.5 17.1 %copy-start.8 = (bf16[32,8192]{1,0:T(8,128)(2,1)S(1)}, bf16[32,8192]{1,0:T(8,128)(2,1)}, u32[]{:S(2)}) copy-start(bf16[32,8192]{1,0:T(8,128)(2,1)} %param.12) | copy-start | bytes 1572868
  51.6 77.2 %collective-permute-start.1 = (f32[1,32,128]{1,2,0:T(8,128)S(1)}, f32[1,32,128]{1,2,0:T(8,128)}, u32[]{:S(2)}, u32[]{:S(2)}) collective-permute-start(f32[1,32,128]{1,2,0:T(8,128)S(1)} %bitcast_select_fusion), channel_id=1, source_target_pairs={{0,4},{4,0},{8,12},{12,8},{16,20},{20,16},{24,28},{28,24},{32,36},... | collective-permute-start | bytes 49160 | tf_op jit(solution)/shard_map/ppermute | solution.py:11
  62.6 12.8 %copy-start.9 = (f32[512,32]{1,0:T(8,128)S(1)}, f32[512,32]{1,0:T(8,128)}, u32[]{:S(2)}) copy-start(f32[512,32]{1,0:T(8,128)} %gather_fusion.3) | copy-start | bytes 196612
  63.4 68.3 %collective-permute-start = (f32[1,32,128]{2,1,0:T(8,128)}, f32[1,32,128]{2,1,0:T(8,128)}, u32[]{:S(2)}, u32[]{:S(2)}) collective-permute-start(f32[1,32,128]{2,1,0:T(8,128)} %bitcast.48), channel_id=1, source_target_pairs={{0,4},{4,0},{8,12},{12,8},{16,20},{20,16},{24,28},{28,24},{32,36},... | collective-permute-start | bytes 49160 | tf_op jit(solution)/shard_map/ppermute | solution.py:11
  66.1 69.7 %collective-permute-start.4 = (f32[1,32,128]{2,1,0:T(8,128)S(1)}, f32[1,32,128]{2,1,0:T(8,128)}, u32[]{:S(2)}, u32[]{:S(2)}) collective-permute-start(f32[1,32,128]{2,1,0:T(8,128)S(1)} %bitcast.455), channel_id=1, source_target_pairs={{0,4},{4,0},{8,12},{12,8},{16,20},{20,16},{24,28},{28,24},{32,36},... | collective-permute-start | bytes 49160 | tf_op jit(solution)/shard_map/ppermute | solution.py:11
  69.4 17.7 %copy-start.5 = (f32[16,32,128]{2,1,0:T(8,128)S(1)}, f32[16,32,128]{2,1,0:T(8,128)}, u32[]{:S(2)}) copy-start(f32[16,32,128]{2,1,0:T(8,128)} %copy-done.4) | copy-start | bytes 786436
  69.4 187.5 %all-to-all-start = ((bf16[32,4,2048]{2,0,1:T(8,128)(2,1)}), bf16[32,4,2048]{2,0,1:T(8,128)(2,1)S(1)}, u32[]{:S(2)}, u32[]{:S(2)}) async-start(bf16[32,4,2048]{2,0,1:T(8,128)(2,1)} %bitcast.446), calls=%async_computation | async-start | bytes 1048576 | tf_op jit(solution)/shard_map/all_to_all | solution.py:116
  73.2 13.9 %copy-start.28 = (pred[16,128]{1,0:T(8,128)(4,1)S(1)}, pred[16,128]{1,0:T(8,128)(4,1)}, u32[]{:S(2)}) copy-start(pred[16,128]{1,0:T(8,128)(4,1)} %copy-done.27) | copy-start | bytes 6148
  118.9 7.5 %copy-start.14 = (f32[128,128]{1,0:T(8,128)S(1)}, f32[128,128]{1,0:T(8,128)}, u32[]{:S(2)}) copy-start(f32[128,128]{1,0:T(8,128)} %fusion.97) | copy-start | bytes 196612
  118.9 8.3 %copy-start.15 = (f32[128,128]{1,0:T(8,128)S(1)}, f32[128,128]{1,0:T(8,128)}, u32[]{:S(2)}) copy-start(f32[128,128]{1,0:T(8,128)} %fusion.91) | copy-start | bytes 196612
  118.9 8.4 %copy-start.13 = (f32[128,128]{1,0:T(8,128)S(1)}, f32[128,128]{1,0:T(8,128)}, u32[]{:S(2)}) copy-start(f32[128,128]{1,0:T(8,128)} %fusion.88) | copy-start | bytes 196612
  129.8 10.8 %collective-permute-start.3 = (f32[2,32,128]{2,1,0:T(8,128)S(1)}, f32[2,32,128]{2,1,0:T(8,128)S(1)}, u32[]{:S(2)}, u32[]{:S(2)}) collective-permute-start(f32[2,32,128]{2,1,0:T(8,128)S(1)} %pad_maximum_fusion.3), channel_id=1, source_target_pairs={{0,8},{4,12},{8,0},{12,4},{16,24},{20,28},{24,16},{28,20},{32,40},... | collective-permute-start | bytes 98312 | tf_op jit(solution)/shard_map/ppermute | solution.py:11
  132.4 123.0 %collective-permute-start.2 = (f32[2,32,128]{2,1,0:T(8,128)S(1)}, f32[2,32,128]{2,1,0:T(8,128)S(1)}, u32[]{:S(2)}, u32[]{:S(2)}) collective-permute-start(f32[2,32,128]{2,1,0:T(8,128)S(1)} %pad_maximum_fusion.2), channel_id=1, source_target_pairs={{0,8},{4,12},{8,0},{12,4},{16,24},{20,28},{24,16},{28,20},{32,40},... | collective-permute-start | bytes 98312 | tf_op jit(solution)/shard_map/ppermute | solution.py:11
  136.5 61.5 %collective-permute-start.5 = (f32[2,32,128]{2,1,0:T(8,128)S(1)}, f32[2,32,128]{2,1,0:T(8,128)S(1)}, u32[]{:S(2)}, u32[]{:S(2)}) collective-permute-start(f32[2,32,128]{2,1,0:T(8,128)S(1)} %pad_maximum_fusion.4), channel_id=1, source_target_pairs={{0,8},{4,12},{8,0},{12,4},{16,24},{20,28},{24,16},{28,20},{32,40},... | collective-permute-start | bytes 98312 | tf_op jit(solution)/shard_map/ppermute | solution.py:11
  198.9 49.7 %copy-start.2 = (f32[32,4096]{0,1:T(8,128)S(1)}, f32[32,4096]{0,1:T(8,128)}, u32[]{:S(2)}) copy-start(f32[32,4096]{0,1:T(8,128)} %copy-done.1) | copy-start | bytes 1572868
  262.7 13.9 %all-to-all-start.1 = ((bf16[4,32,2048]{2,1,0:T(8,128)(2,1)}), bf16[4,32,2048]{2,1,0:T(8,128)(2,1)S(1)}, u32[]{:S(2)}, u32[]{:S(2)}) async-start(bf16[4,32,2048]{2,1,0:T(8,128)(2,1)} %all_to_all.25), calls=%async_computation.1 | async-start | bytes 1048576 | tf_op jit(solution)/shard_map/all_to_all | solution.py:122
  (17 other events, 85.5 us)
where the time goes:
time: 284 us; the launch traced here: 282 us
  blocking collectives  104 us (37%)
  matrix products  65.8 us (23%)
  local copies, waits for them, and re-layouts  56.1 us (20%)
  starting transfers between devices  29 us (10%)
  other arithmetic  18.2 us (6%)
  waiting for transfers between devices  6.9 us (2%)
    all_gather x1, blocking collectives, per_device(): lax.all_gather(send_places, 'leaf', axis=1, tiled=True)  54.5 us
    all_gather x1, blocking collectives, per_device(): lax.all_gather(send_coeffs, 'leaf', axis=1, tiled=True)  49.7 us
    gather x2, local copies, waits for them, and re-layouts, per_device(): jnp.take_along_axis(leaf_points, skeleton_leaf[:, None, :], axis=2)  31.6 us
    dot_general x64, matrix products, kernel_block(): jnp.dot(left.T, right, precision=HIGH, preferred_element_type=jnp.float32)  29.1 us
    ppermute x6, starting transfers between devices, from_partner(): lax.ppermute(shard, axis, [(i, i ^ 1 << apart) for i in range(lax.axis_si...  20.5 us
    dot_general x60, matrix products, per_group(): jnp.dot(group_coeffs[source], kernel_block(group_places[source], group_pl...  15.4 us
    all_to_all x1, waiting for transfers between devices, per_device(): lax.all_to_all(near_flat, 'rhs', split_axis=0, concat_axis=1, tiled=True)  6.88 us
    gather x2, local copies, waits for them, and re-layouts, parent_places(): return jnp.take_along_axis(candidates, index[:, None, :], axis=2)  6.68 us
  transfers between devices with their start and end apart: 8, of which 1 were waited for; matrix products, arithmetic and copies ran while one was open for 27% of the time, Pallas kernels for 0%

commit v1 on v0

v1 whole, which is shorter than its diff:
```python
import jax
import jax.numpy as jnp
from jax import lax
from jax.experimental import pallas as pl
from jax.experimental.pallas import tpu as pltpu
from jax.sharding import PartitionSpec as P

RIDGE = 1.0
SCALE = (2.0 * 1.4426950408889634) ** 0.5
BF = jnp.bfloat16
F32 = jnp.float32
VMEM_LIMIT = 64 * 1024 * 1024 - 131072


def mm(a, b):
    return jnp.dot(a, b, preferred_element_type=F32)


def mm_nt(a, b):
    return lax.dot_general(a, b, (((1,), (1,)), ((), ())), preferred_element_type=F32)


def mm_tn(a, b):
    return lax.dot_general(a, b, (((0,), (0,)), ((), ())), preferred_element_type=F32)


def halves(x):
    hi = x.astype(BF)
    return hi, (x - hi.astype(F32)).astype(BF)


def stacked(x):
    return jnp.concatenate(halves(x), axis=0)


def fold(x):
    rows = x.shape[0] // 2
    return x[:rows] + x[rows:]


def chosen(index, count):
    rows = lax.broadcasted_iota(jnp.int32, (count, index.shape[1]), 0)
    return jnp.where(rows == index, 1.0, 0.0).astype(BF)


def operands(h, m):
    full = h.astype(F32) + m.astype(F32)
    norm = -0.5 * jnp.sum(full * full, axis=0, keepdims=True)
    n1 = norm.astype(BF).astype(F32)
    n2 = (norm - n1).astype(BF).astype(F32)
    n3 = norm - n1 - n2
    row = lax.broadcasted_iota(jnp.int32, (16, h.shape[1]), 0)
    one = jnp.where((row >= 3) & (row < 6), 1.0, 0.0)
    left = jnp.where(row == 0, n1, jnp.where(row == 1, n2, jnp.where(row == 2, n3, one)))
    one = jnp.where(row < 3, 1.0, 0.0)
    right = jnp.where(row == 3, n1, jnp.where(row == 4, n2, jnp.where(row == 5, n3, one)))
    return (
        jnp.concatenate([h, h, m, left.astype(BF)], axis=0),
        jnp.concatenate([h, m, h, right.astype(BF)], axis=0),
    )


def up_kernel(
    rhs, pts, basis, idx_leaf, idx_lower, idx_upper, t_leaf, t_lower, t_upper,
    c0_out, s0_out, c1_out, s1_out, msg_out, c1_all, s1_all,
):
    step = pl.program_id(0)
    coeffs, places = [], []
    for q in range(4):
        cols = slice(512 * q, 512 * (q + 1))
        coeffs.append(mm(rhs[:, cols], basis[q]))
        hm = stacked(pts[:, cols] * SCALE)
        pick = chosen(idx_leaf[pl.ds(4 * step + q, 1), :], 512)
        places.append(mm(hm, pick).astype(BF))
    c0 = jnp.concatenate(coeffs, axis=1)
    s0 = jnp.concatenate(places, axis=1)
    c0_out[...] = c0
    s0_out[...] = s0
    c1 = fold(mm(stacked(c0), t_leaf[...].reshape(512, 128)))
    s1 = mm(s0, chosen(idx_lower[pl.ds(step, 1), :], 512)).astype(BF)
    c1_out[...] = c1
    s1_out[...] = s1
    lanes = pl.ds(pl.multiple_of(step * 128, 128), 128)
    c1_all[:, lanes] = c1
    s1_all[:, lanes] = s1

    @pl.when(step == 3)
    def _():
        c2 = fold(mm(stacked(c1_all[...]), t_lower[...].reshape(512, 128)))
        s2 = mm(s1_all[...], chosen(idx_upper[...], 512)).astype(BF)
        raised = fold(mm(stacked(c2), t_upper[0]))
        msg = jnp.concatenate([c2.astype(BF), stacked(raised), s2], axis=0)
        for k in range(4):
            msg_out[k] = msg


def mid_kernel(got, idx_top, msg_out, place_out, turned):
    position = lax.axis_index("leaf")
    c3 = jnp.zeros((32, 128), F32)
    for k in range(4):
        c3 = c3 + got[k, 32:64, :].astype(F32) + got[k, 64:96, :].astype(F32)
    s2 = jnp.concatenate([got[k, 96:160, :] for k in range(4)], axis=1)
    s3 = mm(s2, chosen(idx_top[pl.ds(position // 4, 1), :], 512))
    place_out[...] = s3.astype(BF)
    hi, lo = halves(c3)
    rows = jnp.concatenate([hi.astype(F32), lo.astype(F32), s3], axis=0)
    turned[...] = rows.T
    quarter = pl.ds(pl.multiple_of((position % 4) * 32, 32), 32)
    msg = turned[quarter, :].astype(BF)
    for k in range(32):
        msg_out[k] = msg


def sibling_sum(c, left, right):
    chl = stacked(c)
    total = []
    for t in range(4):
        out = slice(128 * t, 128 * (t + 1))
        acc = jnp.zeros((32, 128), F32)
        for s in range(4):
            if s == t:
                continue
            src = slice(128 * s, 128 * (s + 1))
            block = jnp.exp2(mm_tn(left[:, src], right[:, out]))
            hi, lo = halves(block)
            acc = acc + fold(mm(chl[:, src], hi)) + mm(chl[:32, src], lo)
        total.append(acc)
    return jnp.concatenate(total, axis=1)


def near_kernel(
    rhs, pts, c0, s0, c1, s1, got, place3,
    near_out, t0_out, t1_out, t2_out,
):
    step = pl.program_id(0)
    for q in range(4):
        base = 512 * q
        x = rhs[:, base:base + 512]
        h, m = halves(pts[:, base:base + 512] * SCALE)
        left, right = operands(h, m)
        for t in range(2):
            out = slice(256 * t, 256 * (t + 1))
            acc = x[:, out].astype(F32) * RIDGE
            total = jnp.zeros((32, 256), F32)
            for s in range(2):
                src = slice(256 * s, 256 * (s + 1))
                block = jnp.exp2(mm_tn(left[:, src], right[:, out])).astype(BF)
                total = total + mm(x[:, src], block)
            near_out[:, base + 256 * t:base + 256 * (t + 1)] = (total + acc).astype(BF)
    t0_out[...] = sibling_sum(c0[...], *operands(s0[:32, :], s0[32:, :]))

    @pl.when(step == 3)
    def _():
        t1_out[...] = sibling_sum(c1[...], *operands(s1[:32, :], s1[32:, :]))
        mine = lax.axis_index("leaf") % 4
        target, _ = operands(got[mine, 96:128, :], got[mine, 128:160, :])
        acc = jnp.zeros((32, 128), F32)
        for k in range(4):
            _, source = operands(got[k, 96:128, :], got[k, 128:160, :])
            block = jnp.exp2(mm_tn(target, source))
            hi, lo = halves(block)
            c2 = jnp.where(mine == k, 0.0, got[k, 0:32, :].astype(F32)).astype(BF)
            acc = acc + mm_nt(c2, hi) + mm_nt(c2, lo)
        t2_out[...] = acc


def top_kernel(got, place3, t2, out):
    node = lax.axis_index("leaf") // 4
    turned = got[...].reshape(1024, 128).T
    column = lax.broadcasted_iota(jnp.int32, (64, 1024), 1)
    c3 = jnp.where(column // 32 == node, 0.0, turned[:64].astype(F32)).astype(BF)
    target, _ = operands(place3[:32, :], place3[32:, :])
    _, source = operands(turned[64:96], turned[96:])
    acc = jnp.zeros((32, 128), F32)
    for k in range(4):
        cols = slice(256 * k, 256 * (k + 1))
        hi, lo = halves(jnp.exp2(mm_tn(target, source[:, cols])))
        acc = acc + fold(mm_nt(c3[:, cols], hi)) + mm_nt(c3[:32, cols], lo)
    for k in range(4):
        out[k] = acc


def down_kernel(
    got, t0, t1, t2, near, basis, t_leaf, t_lower, t_upper,
    out, g1_all,
):
    step = pl.program_id(0)

    @pl.when(step == 0)
    def _():
        t3 = (got[0] + got[1]) + (got[2] + got[3])
        g2 = t2[...] + fold(mm_nt(stacked(t3), t_upper[0]))
        g1_all[...] = t1[...] + fold(mm_nt(stacked(g2), t_lower[...].reshape(512, 128)))

    g1 = g1_all[:, pl.ds(pl.multiple_of(step * 128, 128), 128)]
    g0 = t0[...] + fold(mm_nt(stacked(g1), t_leaf[...].reshape(512, 128)))
    g0 = g0.astype(BF)
    for q in range(4):
        cols = slice(512 * q, 512 * (q + 1))
        far = mm_nt(g0[:, 128 * q:128 * (q + 1)], basis[q])
        out[:, cols] = (near[:, cols].astype(F32) + far).astype(BF)


def whole(shape):
    return pl.BlockSpec(shape, lambda i: (0,) * len(shape))


def params():
    return pltpu.CompilerParams(vmem_limit_bytes=VMEM_LIMIT)


def per_device(
    rhs_block, points, basis, skeleton_leaf, skeleton_lower, skeleton_upper,
    skeleton_top, transfer_leaf, transfer_lower, transfer_upper,
):
    shape = jax.ShapeDtypeStruct
    wide = pl.BlockSpec((32, 2048), lambda i: (0, i))
    leaf_basis = pl.BlockSpec((4, 512, 128), lambda i: (i, 0, 0))
    leaf_transfer = pl.BlockSpec((4, 128, 128), lambda i: (i, 0, 0))

    c0, s0, c1, s1, msg1 = pl.pallas_call(
        up_kernel,
        grid=(4,),
        in_specs=[
            wide, wide, leaf_basis,
            whole((16, 128)), whole((4, 128)), whole((1, 128)),
            leaf_transfer, whole((4, 128, 128)), whole((1, 128, 128)),
        ],
        out_specs=[
            pl.BlockSpec((32, 512), lambda i: (0, i)),
            pl.BlockSpec((64, 512), lambda i: (0, i)),
            pl.BlockSpec((32, 128), lambda i: (0, i)),
            pl.BlockSpec((64, 128), lambda i: (0, i)),
            whole((4, 160, 128)),
        ],
        out_shape=[
            shape((32, 2048), F32), shape((64, 2048), BF),
            shape((32, 512), F32), shape((64, 512), BF),
            shape((4, 160, 128), BF),
        ],
        scratch_shapes=[pltpu.VMEM((32, 512), F32), pltpu.VMEM((64, 512), BF)],
        compiler_params=params(),
        cost_estimate=pl.CostEstimate(flops=10**9, bytes_accessed=5 * 10**6, transcendentals=0),
        name="upward",
    )(rhs_block, points, basis, skeleton_leaf, skeleton_lower, skeleton_upper,
      transfer_leaf, transfer_lower, transfer_upper)

    nodes = lax.axis_size("leaf") // 4
    siblings = [[4 * k + i for i in range(4)] for k in range(nodes)]
    same_place = [[4 * k + i for k in range(nodes)] for i in range(4)]
    got1 = lax.all_to_all(msg1, "leaf", 0, 0, axis_index_groups=siblings, tiled=True)

    msg2, place3 = pl.pallas_call(
        mid_kernel,
        out_shape=[shape((32, 32, 128), BF), shape((64, 128), BF)],
        scratch_shapes=[pltpu.VMEM((128, 128), F32)],
        compiler_params=params(),
        name="middle",
    )(got1, skeleton_top)

    got2 = lax.all_to_all(msg2, "leaf", 0, 0, axis_index_groups=same_place, tiled=True)

    near, t0, t1, t2 = pl.pallas_call(
        near_kernel,
        grid=(4,),
        in_specs=[
            wide, wide,
            pl.BlockSpec((32, 512), lambda i: (0, i)),
            pl.BlockSpec((64, 512), lambda i: (0, i)),
            whole((32, 512)), whole((64, 512)), whole((4, 160, 128)),
            pl.BlockSpec(memory_space=pl.ANY),
        ],
        out_specs=[
            wide, pl.BlockSpec((32, 512), lambda i: (0, i)),
            whole((32, 512)), whole((32, 128)),
        ],
        out_shape=[
            shape((32, 8192), BF), shape((32, 2048), F32),
            shape((32, 512), F32), shape((32, 128), F32),
        ],
        compiler_params=params(),
        cost_estimate=pl.CostEstimate(
            flops=6 * 10**9, bytes_accessed=3 * 10**6, transcendentals=5 * 10**6),
        name="near",
    )(rhs_block, points, c0, s0, c1, s1, got1, place3)

    part = pl.pallas_call(
        top_kernel,
        in_specs=[whole((32, 32, 128)), whole((64, 128)), pl.BlockSpec(memory_space=pl.ANY)],
        out_specs=whole((4, 32, 128)),
        grid=(1,),
        out_shape=shape((4, 32, 128), F32),
        compiler_params=params(),
        name="top",
    )(got2, place3, t2)

    got3 = lax.all_to_all(part, "leaf", 0, 0, axis_index_groups=siblings, tiled=True)

    return pl.pallas_call(
        down_kernel,
        grid=(4,),
        in_specs=[
            whole((4, 32, 128)),
            pl.BlockSpec((32, 512), lambda i: (0, i)),
            whole((32, 512)), whole((32, 128)), wide, leaf_basis,
            leaf_transfer, whole((4, 128, 128)), whole((1, 128, 128)),
        ],
        out_specs=wide,
        out_shape=shape((32, 8192), BF),
        scratch_shapes=[pltpu.VMEM((32, 512), F32)],
        compiler_params=params(),
        cost_estimate=pl.CostEstimate(
            flops=2 * 10**9, bytes_accessed=5 * 10**6, transcendentals=10**6),
        name="downward",
    )(got3, t0, t1, t2, near, basis, transfer_leaf,
      transfer_lower, transfer_upper)


def solution(mesh):
    return jax.shard_map(
        per_device,
        mesh=mesh,
        in_specs=(
            P("rhs", "leaf"),
            P(None, "leaf"),
            P("leaf", None, None),
            P("leaf", None),
            P("leaf", None),
            P("leaf", None),
            P(),
            P("leaf", None, None),
            P("leaf", None, None),
            P("leaf", None, None),
        ),
        out_specs=P("rhs", "leaf"),
        check_vma=False,
    )
```

time: 284 us -> 63.1 us (0.22)
  blocking collectives: 104 us -> 23.4 us
  matrix products: 65.8 us -> 0 us
  local copies, waits for them, and re-layouts: 56.1 us -> 0 us
  Pallas kernels: 0 us -> 28.7 us
  starting transfers between devices: 29 us -> 10.4 us
  other arithmetic: 18.2 us -> 0 us
  waiting for transfers between devices: 6.9 us -> 0.01 us
    all_gather x2 -> x0, blocking collectives: 104 us -> none  [the longest x1 54.5 us: per_device(): lax.all_gather(send_places, 'leaf', axis=1, tiled=True)]
    dot_general x138 -> x0, matrix products: 65.8 us -> none  [the longest x64 29.1 us: kernel_block(): jnp.dot(left.T, right, precision=HIGH, preferred_element_type=jnp.float32)]
    gather x5 -> x0, local copies, waits for them, and re-layouts: 38.9 us -> none  [the longest x2 31.6 us: per_device(): jnp.take_along_axis(leaf_points, skeleton_leaf[:, None, :], axis=2)]
    pallas_call x0 -> x5, Pallas kernels: none -> 28.7 us  [the longest x1 14.5 us: per_device(): pl.pallas_call(near_kernel, grid=(4,), in_specs=[wide, wide, pl.BlockSpec...]
    all_to_all x0 -> x2, blocking collectives: none -> 23.4 us  [the longest x1 15.3 us: per_device(): lax.all_to_all(msg1, 'leaf', 0, 0, axis_index_groups=siblings, tiled=True)]
    ppermute x6 -> x0, starting transfers between devices: 20.5 us -> none  [from_partner(): lax.ppermute(shard, axis, [(i, i ^ 1 << apart) for i in range(lax.axis_si...]
    all_to_all x2 -> x1, waiting for transfers between devices: 6.89 us -> 0.01 us  [per_device(): lax.all_to_all(msg2, 'leaf', 0, 0, axis_index_groups=same_place, tiled=True)]
    reshape x4 -> x0, local copies, waits for them, and re-layouts: 5.03 us -> none  [the longest x1 2.64 us: per_device(): leaf_points = points.reshape(dims, leaves, leaf).transpose(1, 0, 2)]
  transfers between devices with their start and end apart: 8 -> 1, of which waited for: 1 -> 0; matrix products, arithmetic and copies ran while one was open for 27% -> 0% of each run, Pallas kernels for 0% -> 23%
where the time goes in v1:
time: 63.1 us; the launch traced here: 62.6 us
  Pallas kernels  28.7 us (45%)
  blocking collectives  23.4 us (37%)
  starting transfers between devices  10.4 us (16%)
    all_to_all x1, blocking collectives, per_device(): lax.all_to_all(msg1, 'leaf', 0, 0, axis_index_groups=siblings, tiled=True)  15.3 us
    pallas_call x1, Pallas kernels, per_device(): pl.pallas_call(near_kernel, grid=(4,), in_specs=[wide, wide, pl.BlockSpec...  14.5 us
    all_to_all x1, starting transfers between devices, per_device(): lax.all_to_all(msg2, 'leaf', 0, 0, axis_index_groups=same_place, tiled=True)  10.4 us
    all_to_all x1, blocking collectives, per_device(): lax.all_to_all(part, 'leaf', 0, 0, axis_index_groups=siblings, tiled=True)  8.06 us
    pallas_call x1, Pallas kernels, per_device(): pl.pallas_call(up_kernel, grid=(4,), in_specs=[wide, wide, leaf_basis, wh...  5.06 us
    pallas_call x1, Pallas kernels, per_device(): pl.pallas_call(down_kernel, grid=(4,), in_specs=[whole((4, 32, 128)), pl....  4.9 us
    pallas_call x1, Pallas kernels, per_device(): pl.pallas_call(top_kernel, in_specs=[whole((32, 32, 128)), whole((64, 128...  2.32 us
    pallas_call x1, Pallas kernels, per_device(): pl.pallas_call(mid_kernel, out_shape=[shape((32, 32, 128), BF), shape((64...  1.9 us
  transfers between devices with their start and end apart: 1, of which 0 were waited for; matrix products, arithmetic and copies ran while one was open for 0% of the time, Pallas kernels for 23%

profile of v1, /device:TPU:1, one launch (start us, length us, event | category | flops | bytes accessed | tf_op | source)
XLA Modules:
  0.0 62.6 jit_solution(1005163147246897592)
XLA Ops:
  0.0 5.1 %upward.1 = (f32[32,2048]{1,0:T(8,128)}, bf16[64,2048]{1,0:T(8,128)(2,1)}, f32[32,512]{1,0:T(8,128)}, bf16[64,512]{1,0:T(8,128)(2,1)}, bf16[4,160,128]{2,1,0:T(8,128)(2,1)}) custom-call(bf16[32,8192]{1,0:T(8,128)(2,1)} %rhs.3, f32[32,8192]{1,0:T(8,128)} %pts.3, bf16[16,512,128]{2,1,0:T(8,128)(2,1)} %basis.3, s32[16,128]{1,0:T(8,128)} %idx_leaf.1, ...), custom_call_target="tpu_custom_call" | custom-call | flops 1000000000 | bytes 5000000 | tf_op jit(solution)/shard_map/upward/pallas_call | solution.py:221
  5.1 15.3 %all_to_all.15.got = bf16[4,160,128]{2,1,0:T(8,128)(2,1)} all-to-all(bf16[4,160,128]{2,1,0:T(8,128)(2,1)} %get-tuple-element.16), channel_id=1, replica_groups={{0,4,8,12},{16,20,24,28},{32,36,40,44},{48,52,56,60},{64,68,72,76},{80,..., dimensions={0} | all-to-all | bytes 327680 | tf_op jit(solution)/shard_map/all_to_all | solution.py:251
  20.4 1.9 %middle.1 = (bf16[32,32,128]{2,1,0:T(8,128)(2,1)}, bf16[64,128]{1,0:T(8,128)(2,1)}) custom-call(bf16[4,160,128]{2,1,0:T(8,128)(2,1)} %all_to_all.15.got, s32[32,128]{1,0:T(8,128)} %idx_top.1), custom_call_target="tpu_custom_call" | custom-call | tf_op jit(solution)/shard_map/middle/pallas_call | solution.py:253
  22.3 10.4 %all-to-all-start.1 = ((bf16[32,32,128]{2,1,0:T(8,128)(2,1)}), bf16[32,32,128]{2,1,0:T(8,128)(2,1)}, u32[]{:S(2)}, u32[]{:S(2)}) async-start(bf16[32,32,128]{2,1,0:T(8,128)(2,1)} %get-tuple-element.17), calls=%async_computation.1 | async-start | bytes 524288 | tf_op jit(solution)/shard_map/all_to_all | solution.py:261
  32.8 14.5 %near.1 = (bf16[32,8192]{1,0:T(8,128)(2,1)}, f32[32,2048]{1,0:T(8,128)}, f32[32,512]{1,0:T(8,128)}, f32[32,128]{1,0:T(8,128)}) custom-call(bf16[32,8192]{1,0:T(8,128)(2,1)} %rhs.3, f32[32,8192]{1,0:T(8,128)} %pts.3, f32[32,2048]{1,0:T(8,128)} %get-tuple-element.19.c0, bf16[64,2048]{1,0:T(8,128)(2,1)} %get-tuple-element.20.s0, ...), custom_call_target="tpu_custom_call" | custom-call | flops 6000000000 | bytes 3000000 | tf_op jit(solution)/shard_map/near/pallas_call | solution.py:263
  47.3 0.0 all-to-all-done.1.got
  47.3 2.3 %top.1 = f32[4,32,128]{2,1,0:T(8,128)} custom-call(bf16[32,32,128]{2,1,0:T(8,128)(2,1)} %all-to-all-done.1.got, bf16[64,128]{1,0:T(8,128)(2,1)} %get-tuple-element.18.place3, f32[32,128]{1,0:T(8,128)} %get-tuple-element.23.t2), custom_call_target="tpu_custom_call" | custom-call | tf_op jit(solution)/shard_map/top/pallas_call | solution.py:287
  49.6 8.1 %all_to_all.16.got = f32[4,32,128]{2,1,0:T(8,128)} all-to-all(f32[4,32,128]{2,1,0:T(8,128)} %top.1), channel_id=1, replica_groups={{0,4,8,12},{16,20,24,28},{32,36,40,44},{48,52,56,60},{64,68,72,76},{80,..., dimensions={0} | all-to-all | bytes 131072 | tf_op jit(solution)/shard_map/all_to_all | solution.py:297
  57.7 4.9 %downward.1 = bf16[32,8192]{1,0:T(8,128)(2,1)} custom-call(f32[4,32,128]{2,1,0:T(8,128)} %all_to_all.16.got, f32[32,2048]{1,0:T(8,128)} %get-tuple-element.24.t0, f32[32,512]{1,0:T(8,128)} %get-tuple-element.25.t1, f32[32,128]{1,0:T(8,128)} %get-tuple-element.23.t2, bf16[32,8192]{1,0:T(8,128)(2,1)} %get-tuple-element.26.near, bf16[16,512,128]{2,1,0:T(8,128)(2,1)} %basis.3, ...), custom_call_target="tpu_custom_call" | custom-call | flops 2000000000 | bytes 5000000 | tf_op jit(solution)/shard_map/downward/pallas_call | solution.py:299
Async XLA Ops:
  22.3 25.0 %all-to-all-start.1 = ((bf16[32,32,128]{2,1,0:T(8,128)(2,1)}), bf16[32,32,128]{2,1,0:T(8,128)(2,1)}, u32[]{:S(2)}, u32[]{:S(2)}) async-start(bf16[32,32,128]{2,1,0:T(8,128)(2,1)} %get-tuple-element.17), calls=%async_computation.1 | async-start | bytes 524288 | tf_op jit(solution)/shard_map/all_to_all | solution.py:261

commit v2 on v1

v2 whole, which is shorter than its diff:
```python
import jax
import jax.numpy as jnp
from jax import lax
from jax.experimental import pallas as pl
from jax.experimental.pallas import tpu as pltpu
from jax.sharding import PartitionSpec as P

RIDGE = 1.0
SCALE = (2.0 * 1.4426950408889634) ** 0.5
BF = jnp.bfloat16
F32 = jnp.float32
VMEM_LIMIT = 32 * 1024 * 1024


def mm(a, b):
    return jnp.dot(a, b, preferred_element_type=F32)


def mm_nt(a, b):
    return lax.dot_general(a, b, (((1,), (1,)), ((), ())), preferred_element_type=F32)


def mm_tn(a, b):
    return lax.dot_general(a, b, (((0,), (0,)), ((), ())), preferred_element_type=F32)


def halves(x):
    hi = x.astype(BF)
    return hi, (x - hi.astype(F32)).astype(BF)


def stacked(x):
    return jnp.concatenate(halves(x), axis=0)


def fold(x):
    rows = x.shape[0] // 2
    return x[:rows] + x[rows:]


def chosen(index, count):
    rows = lax.broadcasted_iota(jnp.int32, (count, index.shape[1]), 0)
    return jnp.where(rows == index, 1.0, 0.0).astype(BF)


def operands(h, m):
    full = h.astype(F32) + m.astype(F32)
    norm = -0.5 * jnp.sum(full * full, axis=0, keepdims=True)
    n1 = norm.astype(BF).astype(F32)
    n2 = (norm - n1).astype(BF).astype(F32)
    n3 = norm - n1 - n2
    row = lax.broadcasted_iota(jnp.int32, (16, h.shape[1]), 0)
    one = jnp.where((row >= 3) & (row < 6), 1.0, 0.0)
    left = jnp.where(row == 0, n1, jnp.where(row == 1, n2, jnp.where(row == 2, n3, one)))
    one = jnp.where(row < 3, 1.0, 0.0)
    right = jnp.where(row == 3, n1, jnp.where(row == 4, n2, jnp.where(row == 5, n3, one)))
    return (
        jnp.concatenate([h, h, m, left.astype(BF)], axis=0),
        jnp.concatenate([h, m, h, right.astype(BF)], axis=0),
    )


def copies(pairs, sems, start=0):
    return [
        pltpu.make_async_copy(src, dst, sems.at[start + k])
        for k, (src, dst) in enumerate(pairs)
    ]


def up_kernel(
    rhs, pts, basis, idx_leaf, idx_lower, idx_upper, idx_top, t_leaf, t_lower, t_upper,
    it_v, c0_v, s0_v, c1_v, s1_v, msg_v,
    rhs_v, pts_v, basis_v, tl_v, tlo_v, tu_v, il_v, ilo_v, iu_v, sems, chunk_sems,
):
    small = copies(
        [
            (idx_leaf, il_v), (idx_lower, ilo_v), (idx_upper, iu_v), (t_lower, tlo_v),
            (t_upper, tu_v), (idx_top, it_v),
        ], sems)

    def arrivals(step):
        cols = pl.ds(pl.multiple_of(step * 2048, 2048), 2048)
        leaves = pl.ds(step * 4, 4)
        return copies(
            [
                (pts.at[:, cols], pts_v.at[step]), (rhs.at[:, cols], rhs_v.at[step]),
                (basis.at[leaves], basis_v.at[step]), (t_leaf.at[leaves], tl_v.at[step]),
            ], chunk_sems, 4 * step)

    small[0].start()
    for step in range(4):
        for copy in arrivals(step):
            copy.start()
        if step == 0:
            for copy in small[1:]:
                copy.start()
    small[0].wait()
    small[1].wait()

    def chunk(step, carry):
        for copy in arrivals(step):
            copy.wait()
        coeffs, places = [], []
        for q in range(4):
            cols = slice(512 * q, 512 * (q + 1))
            coeffs.append(mm(rhs_v[step, :, cols], basis_v[step, q]))
            hm = stacked(pts_v[step, :, cols] * SCALE)
            pick = chosen(il_v[pl.ds(4 * step + q, 1), :], 512)
            places.append(mm(hm, pick).astype(BF))
        c0 = jnp.concatenate(coeffs, axis=1)
        s0 = jnp.concatenate(places, axis=1)
        c0_v[step] = c0
        s0_v[step] = s0
        c1 = fold(mm(stacked(c0), tl_v[step].reshape(512, 128)))
        s1 = mm(s0, chosen(ilo_v[pl.ds(step, 1), :], 512)).astype(BF)
        lanes = pl.ds(pl.multiple_of(step * 128, 128), 128)
        c1_v[:, lanes] = c1
        s1_v[:, lanes] = s1
        return carry

    lax.fori_loop(0, 4, chunk, 0)
    for copy in small[2:]:
        copy.wait()
    c2 = fold(mm(stacked(c1_v[...]), tlo_v[...].reshape(512, 128)))
    s2 = mm(s1_v[...], chosen(iu_v[...], 512)).astype(BF)
    raised = fold(mm(stacked(c2), tu_v[0]))
    msg = jnp.concatenate([c2.astype(BF), stacked(raised), s2], axis=0)
    for k in range(4):
        msg_v[k] = msg


def mid_kernel(got, idx_top, msg_out, place_out):
    position = lax.axis_index("leaf")
    c3 = jnp.zeros((32, 128), F32)
    for k in range(4):
        c3 = c3 + got[k, 32:64, :].astype(F32) + got[k, 64:96, :].astype(F32)
    s2 = jnp.concatenate([got[k, 96:160, :] for k in range(4)], axis=1)
    s3 = mm(s2, chosen(idx_top[pl.ds(position // 4, 1), :], 512))
    place_out[...] = s3.astype(BF)
    rows = jnp.concatenate([c3, s3], axis=0)
    moved = pltpu.roll(rows, 64, 1)
    low = lax.broadcasted_iota(jnp.int32, (48, 128), 1) < 64
    first = position % 2 == 0
    msg = jnp.where(
        low,
        jnp.where(first, rows[:48], moved[:48]),
        jnp.where(first, moved[48:], rows[48:]),
    ).astype(BF)
    for k in range(32):
        msg_out[k] = msg


def sibling_sum(c, left, right):
    chl = stacked(c)
    block = jnp.exp2(mm_tn(left, right))
    zero = jnp.zeros((128, 128), F32)
    rows = []
    for s in range(4):
        src = slice(128 * s, 128 * (s + 1))
        rows.append(jnp.concatenate(
            [zero if s == t else block[src, 128 * t:128 * (t + 1)] for t in range(4)], axis=1))
    hi, lo = halves(jnp.concatenate(rows, axis=0))
    return fold(mm(chl, hi)) + mm(chl[:32], lo)


def near_kernel(
    rhs, pts, basis, t_lower, t_upper, c0, s0, c1, s1, got, place3,
    near_out, t0_out, t1_out, t2_out, basis_out, above_out,
    rhs_v, pts_v, near_v, t0_v, sems, chunk_sems, out_sems,
):
    ahead = copies(
        [
            (basis, basis_out), (t_lower, above_out.at[pl.ds(0, 4)]),
            (t_upper, above_out.at[pl.ds(4, 1)]),
        ], sems)

    def arrivals(step):
        cols = pl.ds(pl.multiple_of(step * 2048, 2048), 2048)
        return copies(
            [(pts.at[:, cols], pts_v.at[step]), (rhs.at[:, cols], rhs_v.at[step])],
            chunk_sems, 2 * step)

    def departures(step):
        return copies(
            [(near_v.at[step], near_out.at[step]), (t0_v.at[step], t0_out.at[step])],
            out_sems, 2 * step)

    for step in range(4):
        for copy in arrivals(step):
            copy.start()
    for copy in ahead:
        copy.start()

    def chunk(step, carry):
        for copy in arrivals(step):
            copy.wait()
        for q in range(4):
            leaf = slice(512 * q, 512 * (q + 1))
            x = rhs_v[step, :, leaf]
            left, right = operands(*halves(pts_v[step, :, leaf] * SCALE))
            wide = jnp.exp2(mm_tn(left[:, :256], right)).astype(BF)
            last = jnp.exp2(mm_tn(left[:, 256:], right[:, 256:])).astype(BF)
            both = mm(x[:, :256], wide) + RIDGE * x.astype(F32)
            first = both[:, :256] + mm_nt(x[:, 256:], wide[:, 256:])
            second = both[:, 256:] + mm(x[:, 256:], last)
            near_v[step, :, leaf] = jnp.concatenate([first, second], axis=1).astype(BF)
        t0_v[step] = sibling_sum(c0[step], *operands(s0[step, :32, :], s0[step, 32:, :]))
        for copy in departures(step):
            copy.start()
        return carry

    lax.fori_loop(0, 4, chunk, 0)
    t1_out[...] = sibling_sum(c1[...], *operands(s1[:32, :], s1[32:, :]))
    mine = lax.axis_index("leaf") % 4
    target, _ = operands(got[mine, 96:128, :], got[mine, 128:160, :])

    def side(rows):
        return jnp.concatenate([got[k, rows, :] for k in range(4)], axis=1)

    _, source = operands(side(slice(96, 128)), side(slice(128, 160)))
    hi, lo = halves(jnp.exp2(mm_tn(target, source)))
    c2 = jnp.concatenate(
        [jnp.where(mine == k, 0.0, got[k, 0:32, :].astype(F32)) for k in range(4)], axis=1
    ).astype(BF)
    t2_out[...] = mm_nt(c2, hi) + mm_nt(c2, lo)
    for copy in ahead:
        copy.wait()
    for step in range(4):
        for copy in departures(step):
            copy.wait()


def top_kernel(got, place3, t2, out):
    node = lax.axis_index("leaf") // 4
    target, _ = operands(place3[:32, :], place3[32:, :])
    low = lax.broadcasted_iota(jnp.int32, (48, 128), 1) < 64
    column = lax.broadcasted_iota(jnp.int32, (32, 512), 1)
    acc = jnp.zeros((32, 128), F32)
    for first in range(0, 32, 8):
        parts = []
        for k in range(first, first + 8, 2):
            even, odd = got[k].astype(F32), got[k + 1].astype(F32)
            parts.append(jnp.concatenate([
                jnp.where(low, even, pltpu.roll(odd, 64, 1)),
                jnp.where(low, pltpu.roll(even, 64, 1), odd),
            ], axis=0))
        rows = jnp.concatenate(parts, axis=1)
        c3 = jnp.where(column // 64 == node - first, 0.0, rows[:32]).astype(BF)
        _, source = operands(rows[32:64].astype(BF), rows[64:].astype(BF))
        hi, lo = halves(jnp.exp2(mm_tn(target, source)))
        acc = acc + mm_nt(c3, hi) + mm_nt(c3, lo)
    out[...] = acc


def down_kernel(
    part, other, t0, t1, t2, near, basis, t_leaf, above,
    out, near_v, t0_v, tl_v, out_v, in_sems, out_sems,
):
    arrivals = copies(
        [(t0, t0_v), (t_leaf, tl_v)] + [(near.at[k], near_v.at[k]) for k in range(4)], in_sems)
    for copy in arrivals:
        copy.start()

    def departure(step):
        cols = pl.ds(pl.multiple_of(step * 2048, 2048), 2048)
        return pltpu.make_async_copy(out_v.at[step], out.at[:, cols], out_sems.at[step])

    t3 = part[...] + other[...]
    g2 = t2[...] + fold(mm_nt(stacked(t3), above[4]))
    g1 = t1[...] + fold(mm_nt(stacked(g2), above[:4].reshape(512, 128)))
    for copy in arrivals[:2]:
        copy.wait()
    g0 = []
    for step in range(4):
        here = stacked(g1[:, 128 * step:128 * (step + 1)])
        g0.append((t0_v[step] + fold(mm_nt(here, tl_v[4 * step:4 * step + 4].reshape(512, 128)))).astype(BF))
    for step in range(4):
        arrivals[2 + step].wait()
        for q in range(4):
            cols = slice(512 * q, 512 * (q + 1))
            far = mm_nt(g0[step][:, 128 * q:128 * (q + 1)], basis[4 * step + q])
            out_v[step, :, cols] = (near_v[step, :, cols].astype(F32) + far).astype(BF)
        departure(step).start()
    for step in range(4):
        departure(step).wait()


def call(kernel, name, ins, outs, scratch=(), cost=None, **kwargs):
    spec = lambda space: pl.BlockSpec(memory_space=space)
    return pl.pallas_call(
        kernel,
        in_specs=[spec(space) for _, space in ins],
        out_specs=[spec(space) for _, _, space in outs],
        out_shape=[
            (space if space is not pl.ANY else jax.ShapeDtypeStruct)(shape, dtype)
            for shape, dtype, space in outs
        ],
        scratch_shapes=list(scratch),
        compiler_params=pltpu.CompilerParams(vmem_limit_bytes=VMEM_LIMIT),
        cost_estimate=cost,
        name=name,
    )(*[pltpu.with_memory_space_constraint(x, space) for x, space in ins])


def per_device(
    rhs_block, points, basis, skeleton_leaf, skeleton_lower, skeleton_upper,
    skeleton_top, transfer_leaf, transfer_lower, transfer_upper,
):
    vmem, hbm, dma = pltpu.VMEM, pltpu.HBM, pltpu.SemaphoreType.DMA
    i32 = jnp.int32

    def inside(*arrays):
        return [(x, vmem) for x in arrays]

    def outside(*arrays):
        return [(x, hbm) for x in arrays]

    transfers = (transfer_leaf, transfer_lower, transfer_upper)
    top_index, c0, s0, c1, s1, msg1 = call(
        up_kernel, "upward",
        outside(
            rhs_block, points, basis, skeleton_leaf, skeleton_lower, skeleton_upper,
            skeleton_top, *transfers),
        [
            ((32, 128), i32, vmem), ((4, 32, 512), F32, vmem), ((4, 64, 512), BF, vmem),
            ((32, 512), F32, vmem), ((64, 512), BF, vmem), ((4, 160, 128), BF, vmem),
        ],
        [
            vmem((4, 32, 2048), BF), vmem((4, 32, 2048), F32), vmem((4, 4, 512, 128), BF),
            vmem((4, 4, 128, 128), BF), vmem((4, 128, 128), BF), vmem((1, 128, 128), BF),
            vmem((16, 128), i32), vmem((4, 128), i32), vmem((1, 128), i32),
            dma((6,)), dma((16,)),
        ],
        pl.CostEstimate(flops=10**9, bytes_accessed=5 * 10**6, transcendentals=0),
    )

    nodes = lax.axis_size("leaf") // 4
    siblings = [[4 * k + i for i in range(4)] for k in range(nodes)]
    turn = (0, 0, 1, 1)
    across = [
        [4 * k + 2 * (turn[k % 4] ^ chip) + core for k in range(nodes)]
        for chip in range(2) for core in range(2)
    ]
    got1 = lax.all_to_all(msg1, "leaf", 0, 0, axis_index_groups=siblings, tiled=True)

    msg2, place3 = call(
        mid_kernel, "middle", inside(got1, top_index),
        [((32, 48, 128), BF, vmem), ((64, 128), BF, vmem)],
    )

    got2 = lax.all_to_all(msg2, "leaf", 0, 0, axis_index_groups=across, tiled=True)

    near, t0, t1, t2, gens, above = call(
        near_kernel, "near",
        outside(rhs_block, points, basis, transfer_lower, transfer_upper)
        + inside(c0, s0, c1, s1, got1, place3),
        [
            ((4, 32, 2048), BF, hbm), ((4, 32, 512), F32, hbm),
            ((32, 512), F32, vmem), ((32, 128), F32, vmem),
            ((16, 512, 128), BF, vmem), ((5, 128, 128), BF, vmem),
        ],
        [
            vmem((4, 32, 2048), BF), vmem((4, 32, 2048), F32), vmem((4, 32, 2048), BF),
            vmem((4, 32, 512), F32), dma((3,)), dma((8,)), dma((8,)),
        ],
        pl.CostEstimate(flops=6 * 10**9, bytes_accessed=3 * 10**6, transcendentals=5 * 10**6),
    )

    part, = call(
        top_kernel, "top", inside(got2, place3, t2), [((32, 128), F32, vmem)])

    partner = [(i, i ^ 1) for i in range(4 * nodes)]
    other = lax.ppermute(part, "leaf", partner)

    product, = call(
        down_kernel, "downward",
        inside(part, other) + outside(t0) + inside(t1, t2) + outside(near)
        + inside(gens) + outside(transfer_leaf) + inside(above),
        [((32, 8192), BF, hbm)],
        [
            vmem((4, 32, 2048), BF), vmem((4, 32, 512), F32), vmem((16, 128, 128), BF),
            vmem((4, 32, 2048), BF), dma((6,)), dma((4,)),
        ],
        pl.CostEstimate(flops=2 * 10**9, bytes_accessed=5 * 10**6, transcendentals=10**6),
    )
    return product


def solution(mesh):
    return jax.shard_map(
        per_device,
        mesh=mesh,
        in_specs=(
            P("rhs", "leaf"),
            P(None, "leaf"),
            P("leaf", None, None),
            P("leaf", None),
            P("leaf", None),
            P("leaf", None),
            P(),
            P("leaf", None, None),
            P("leaf", None, None),
            P("leaf", None, None),
        ),
        out_specs=P("rhs", "leaf"),
        check_vma=False,
    )
```

time: 63.1 us -> 53.8 us (0.85)
  the two profiles are of different devices: /device:TPU:1 before, /device:TPU:65 now
where the time goes in v2:
time: 53.8 us; the launch traced here: 53.5 us
  Pallas kernels  18.1 us (34%)
  starting transfers between devices  16.4 us (30%)
  blocking collectives  10.8 us (20%)
  waiting for transfers between devices  6.74 us (13%)
  local copies, waits for them, and re-layouts  1.45 us (3%)
    pallas_call x5, Pallas kernels, call(): pl.pallas_call(kernel, in_specs=[spec(space) for _, space in ins], out_sp...  18.1 us
    all_to_all x1, starting transfers between devices, per_device(): lax.all_to_all(msg2, 'leaf', 0, 0, axis_index_groups=across, tiled=True)  11.6 us
    all_to_all x1, blocking collectives, per_device(): lax.all_to_all(msg1, 'leaf', 0, 0, axis_index_groups=siblings, tiled=True)  10.8 us
    all_to_all x1, waiting for transfers between devices, per_device(): lax.all_to_all(msg2, 'leaf', 0, 0, axis_index_groups=across, tiled=True)  5.92 us
    ppermute x1, starting transfers between devices, per_device(): other = lax.ppermute(part, 'leaf', partner)  4.79 us
    unnamed x4, local copies, waits for them, and re-layouts  1.45 us
  transfers between devices with their start and end apart: 2, of which 2 were waited for; matrix products, arithmetic and copies ran while one was open for 0% of the time, Pallas kernels for 16%

profile of v2, /device:TPU:65, one launch (start us, length us, event | category | flops | bytes accessed | tf_op | source)
XLA Modules:
  0.0 53.5 jit_solution(10382400146479571365)
XLA Ops:
  0.0 3.9 %upward.1 = (s32[32,128]{1,0:T(8,128)S(1)}, f32[4,32,512]{2,1,0:T(8,128)S(1)}, bf16[4,64,512]{2,1,0:T(8,128)(2,1)S(1)}, f32[32,512]{1,0:T(8,128)S(1)}, bf16[64,5...) custom-call(bf16[32,8192]{1,0:T(8,128)(2,1)} %rhs.3, f32[32,8192]{1,0:T(8,128)} %pts.3, bf16[16,512,128]{2,1,0:T(8,128)(2,1)} %basis.3, ...), custom_call_target="tpu_custom_call" | custom-call | flops 1000000000 | bytes 5000000 | tf_op jit(solution)/shard_map/upward/pallas_call | solution.py:290
  3.9 10.8 %all_to_all.10.got = bf16[4,160,128]{2,1,0:T(8,128)(2,1)S(1)} all-to-all(bf16[4,160,128]{2,1,0:T(8,128)(2,1)S(1)} %get-tuple-element.19), channel_id=1, replica_groups={{0,4,8,12},{16,20,24,28},{32,36,40,44},{48,52,56,60},{64,68,72,76},{80,..., dimensions={0} | all-to-all | bytes 327680 | tf_op jit(solution)/shard_map/all_to_all | solution.py:344
  14.7 1.0 %middle.1 = (bf16[32,48,128]{2,1,0:T(8,128)(2,1)}, bf16[64,128]{1,0:T(8,128)(2,1)S(1)}) custom-call(bf16[4,160,128]{2,1,0:T(8,128)(2,1)S(1)} %all_to_all.10.got, s32[32,128]{1,0:T(8,128)S(1)} %get-tuple-element.20.idx_top), custom_call_target="tpu_custom_call" | custom-call | tf_op jit(solution)/shard_map/middle/pallas_call | solution.py:290
  15.7 11.6 %all-to-all-start.1 = ((bf16[32,48,128]{2,1,0:T(8,128)(2,1)}), bf16[32,48,128]{2,1,0:T(8,128)(2,1)S(1)}, u32[]{:S(2)}, u32[]{:S(2)}) async-start(bf16[32,48,128]{2,1,0:T(8,128)(2,1)} %get-tuple-element.21), calls=%async_computation.1 | async-start | bytes 786432 | tf_op jit(solution)/shard_map/all_to_all | solution.py:351
  27.3 8.7 %near.1 = (bf16[4,32,2048]{2,1,0:T(8,128)(2,1)}, f32[4,32,512]{2,1,0:T(8,128)}, f32[32,512]{1,0:T(8,128)S(1)}, f32[32,128]{1,0:T(8,128)S(1)}, bf16[16,512,128]{2...) custom-call(bf16[32,8192]{1,0:T(8,128)(2,1)} %rhs.3, f32[32,8192]{1,0:T(8,128)} %pts.3, bf16[16,512,128]{2,1,0:T(8,128)(2,1)} %basis.3, ...), custom_call_target="tpu_custom_call" | custom-call | flops 6000000000 | bytes 3000000 | tf_op jit(solution)/shard_map/near/pallas_call | solution.py:290
  36.0 0.0 copy-start
  36.0 0.6 %copy-done = f32[32,512]{1,0:T(8,128)} copy-done((f32[32,512]{1,0:T(8,128)}, f32[32,512]{1,0:T(8,128)S(1)}, u32[]{:S(2)}) %copy-start) | copy-done | bytes 65560
  36.6 5.9 %all-to-all-done.1.got = bf16[32,48,128]{2,1,0:T(8,128)(2,1)S(1)} async-done(((bf16[32,48,128]{2,1,0:T(8,128)(2,1)}), bf16[32,48,128]{2,1,0:T(8,128)(2,1)S(1)}, u32[]{:S(2)}, u32[]{:S(2)}) %all-to-all-start.1) | async-done | bytes 393248 | tf_op jit(solution)/shard_map/all_to_all | solution.py:351
  42.5 1.2 %top.1.part = f32[32,128]{1,0:T(8,128)S(1)} custom-call(bf16[32,48,128]{2,1,0:T(8,128)(2,1)S(1)} %all-to-all-done.1.got, bf16[64,128]{1,0:T(8,128)(2,1)S(1)} %get-tuple-element.22.place3, f32[32,128]{1,0:T(8,128)S(1)} %get-tuple-element.27.t2), custom_call_target="tpu_custom_call" | custom-call | tf_op jit(solution)/shard_map/top/pallas_call | solution.py:290
  43.7 4.8 %collective-permute-start = (f32[32,128]{1,0:T(8,128)S(1)}, f32[32,128]{1,0:T(8,128)S(1)}, u32[]{:S(2)}, u32[]{:S(2)}) collective-permute-start(f32[32,128]{1,0:T(8,128)S(1)} %top.1.part), channel_id=1, source_target_pairs={{0,4},{4,0},{8,12},{12,8},{16,20},{20,16},{24,28},{28,24},{32,36},... | collective-permute-start | bytes 49160 | tf_op jit(solution)/shard_map/ppermute | solution.py:373
  48.5 0.8 %collective-permute-done.other = f32[32,128]{1,0:T(8,128)S(1)} collective-permute-done((f32[32,128]{1,0:T(8,128)S(1)}, f32[32,128]{1,0:T(8,128)S(1)}, u32[]{:S(2)}, u32[]{:S(2)}) %collective-permute-start) | collective-permute-done | bytes 16416 | tf_op jit(solution)/shard_map/ppermute | solution.py:373
  49.3 0.0 copy-start.1
  49.3 0.8 %copy-done.1 = f32[32,512]{1,0:T(8,128)S(1)} copy-done((f32[32,512]{1,0:T(8,128)S(1)}, f32[32,512]{1,0:T(8,128)}, u32[]{:S(2)}) %copy-start.1) | copy-done | bytes 65560
  50.1 3.3 %downward.1 = bf16[32,8192]{1,0:T(8,128)(2,1)} custom-call(f32[32,128]{1,0:T(8,128)S(1)} %top.1.part, f32[32,128]{1,0:T(8,128)S(1)} %collective-permute-done.other, f32[4,32,512]{2,1,0:T(8,128)} %get-tuple-element.28.t0, f32[32,512]{1,0:T(8,128)S(1)} %copy-done.1, f32[32,128]{1,0:T(8,128)S(1)} %get-tuple-element.27.t2, ...), custom_call_target="tpu_custom_call" | custom-call | flops 2000000000 | bytes 5000000 | tf_op jit(solution)/shard_map/downward/pallas_call | solution.py:290
Async XLA Ops:
  15.7 26.8 %all-to-all-start.1 = ((bf16[32,48,128]{2,1,0:T(8,128)(2,1)}), bf16[32,48,128]{2,1,0:T(8,128)(2,1)S(1)}, u32[]{:S(2)}, u32[]{:S(2)}) async-start(bf16[32,48,128]{2,1,0:T(8,128)(2,1)} %get-tuple-element.21), calls=%async_computation.1 | async-start | bytes 786432 | tf_op jit(solution)/shard_map/all_to_all | solution.py:351
  36.0 0.6 %copy-start = (f32[32,512]{1,0:T(8,128)}, f32[32,512]{1,0:T(8,128)S(1)}, u32[]{:S(2)}) copy-start(f32[32,512]{1,0:T(8,128)S(1)} %get-tuple-element.29.t1) | copy-start | bytes 196612
  43.7 5.6 %collective-permute-start = (f32[32,128]{1,0:T(8,128)S(1)}, f32[32,128]{1,0:T(8,128)S(1)}, u32[]{:S(2)}, u32[]{:S(2)}) collective-permute-start(f32[32,128]{1,0:T(8,128)S(1)} %top.1.part), channel_id=1, source_target_pairs={{0,4},{4,0},{8,12},{12,8},{16,20},{20,16},{24,28},{28,24},{32,36},... | collective-permute-start | bytes 49160 | tf_op jit(solution)/shard_map/ppermute | solution.py:373
  49.3 0.8 %copy-start.1 = (f32[32,512]{1,0:T(8,128)S(1)}, f32[32,512]{1,0:T(8,128)}, u32[]{:S(2)}) copy-start(f32[32,512]{1,0:T(8,128)} %copy-done) | copy-start | bytes 196612

commit v3 on v2

--- a/solution.py
+++ b/solution.py
@@ -69,8 +69,9 @@
 
 def up_kernel(
     rhs, pts, basis, idx_leaf, idx_lower, idx_upper, idx_top, t_leaf, t_lower, t_upper,
-    it_v, c0_v, s0_v, c1_v, s1_v, msg_v,
-    rhs_v, pts_v, basis_v, tl_v, tlo_v, tu_v, il_v, ilo_v, iu_v, sems, chunk_sems,
+    it_v, c0_out, s0_out, c1_v, s1_v, msg_v,
+    rhs_v, pts_v, basis_v, tl_v, tlo_v, tu_v, il_v, ilo_v, iu_v,
+    c0_v, s0_v, sems, chunk_sems, out_sems,
 ):
     small = copies(
         [
@@ -86,6 +87,11 @@
                 (pts.at[:, cols], pts_v.at[step]), (rhs.at[:, cols], rhs_v.at[step]),
                 (basis.at[leaves], basis_v.at[step]), (t_leaf.at[leaves], tl_v.at[step]),
             ], chunk_sems, 4 * step)
+
+    def departures(step):
+        return copies(
+            [(c0_v.at[step], c0_out.at[step]), (s0_v.at[step], s0_out.at[step])],
+            out_sems, 2 * step)
 
     small[0].start()
     for step in range(4):
@@ -111,14 +117,15 @@
         s0 = jnp.concatenate(places, axis=1)
         c0_v[step] = c0
         s0_v[step] = s0
-        c1 = fold(mm(stacked(c0), tl_v[step].reshape(512, 128)))
-        s1 = mm(s0, chosen(ilo_v[pl.ds(step, 1), :], 512)).astype(BF)
-        lanes = pl.ds(pl.multiple_of(step * 128, 128), 128)
-        c1_v[:, lanes] = c1
-        s1_v[:, lanes] = s1
+        for copy in departures(step):
+            copy.start()
         return carry
 
     lax.fori_loop(0, 4, chunk, 0)
+    for n in range(4):
+        lanes = slice(128 * n, 128 * (n + 1))
+        c1_v[:, lanes] = fold(mm(stacked(c0_v[n]), tl_v[n].reshape(512, 128)))
+        s1_v[:, lanes] = mm(s0_v[n], chosen(ilo_v[n:n + 1, :], 512)).astype(BF)
     for copy in small[2:]:
         copy.wait()
     c2 = fold(mm(stacked(c1_v[...]), tlo_v[...].reshape(512, 128)))
@@ -127,6 +134,9 @@
     msg = jnp.concatenate([c2.astype(BF), stacked(raised), s2], axis=0)
     for k in range(4):
         msg_v[k] = msg
+    for step in range(4):
+        for copy in departures(step):
+            copy.wait()
 
 
 def mid_kernel(got, idx_top, msg_out, place_out):
@@ -166,24 +176,25 @@
 def near_kernel(
     rhs, pts, basis, t_lower, t_upper, c0, s0, c1, s1, got, place3,
     near_out, t0_out, t1_out, t2_out, basis_out, above_out,
-    rhs_v, pts_v, near_v, t0_v, sems, chunk_sems, out_sems,
+    rhs_v, pts_v, basis_v, c0_v, s0_v, near_v, sems, chunk_sems, out_sems,
 ):
     ahead = copies(
         [
-            (basis, basis_out), (t_lower, above_out.at[pl.ds(0, 4)]),
+            (t_lower, above_out.at[pl.ds(0, 4)]),
             (t_upper, above_out.at[pl.ds(4, 1)]),
         ], sems)
 
     def arrivals(step):
         cols = pl.ds(pl.multiple_of(step * 2048, 2048), 2048)
         return copies(
-            [(pts.at[:, cols], pts_v.at[step]), (rhs.at[:, cols], rhs_v.at[step])],
-            chunk_sems, 2 * step)
-
-    def departures(step):
-        return copies(
-            [(near_v.at[step], near_out.at[step]), (t0_v.at[step], t0_out.at[step])],
-            out_sems, 2 * step)
+            [
+                (pts.at[:, cols], pts_v.at[step]), (rhs.at[:, cols], rhs_v.at[step]),
+                (c0.at[step], c0_v.at[step]), (s0.at[step], s0_v.at[step]),
+                (basis.at[pl.ds(step * 4, 4)], basis_v.at[step]),
+            ], chunk_sems, 5 * step)
+
+    def departure(step):
+        return pltpu.make_async_copy(near_v.at[step], near_out.at[step], out_sems.at[step])
 
     for step in range(4):
         for copy in arrivals(step):
@@ -204,9 +215,10 @@
             first = both[:, :256] + mm_nt(x[:, 256:], wide[:, 256:])
             second = both[:, 256:] + mm(x[:, 256:], last)
             near_v[step, :, leaf] = jnp.concatenate([first, second], axis=1).astype(BF)
-        t0_v[step] = sibling_sum(c0[step], *operands(s0[step, :32, :], s0[step, 32:, :]))
-        for copy in departures(step):
-            copy.start()
+        departure(step).start()
+        for q in range(4):
+            basis_out[4 * step + q] = basis_v[step, q].T
+        t0_out[step] = sibling_sum(c0_v[step], *operands(s0_v[step, :32, :], s0_v[step, 32:, :]))
         return carry
 
     lax.fori_loop(0, 4, chunk, 0)
@@ -226,11 +238,13 @@
     for copy in ahead:
         copy.wait()
     for step in range(4):
-        for copy in departures(step):
-            copy.wait()
-
-
-def top_kernel(got, place3, t2, out):
+        departure(step).wait()
+
+
+def top_kernel(got, place3, near, t_leaf, out, near_out, tl_out, sems):
+    ahead = copies([(t_leaf, tl_out), (near, near_out)], sems)
+    for copy in ahead:
+        copy.start()
     node = lax.axis_index("leaf") // 4
     target, _ = operands(place3[:32, :], place3[32:, :])
     low = lax.broadcasted_iota(jnp.int32, (48, 128), 1) < 64
@@ -250,17 +264,14 @@
         hi, lo = halves(jnp.exp2(mm_tn(target, source)))
         acc = acc + mm_nt(c3, hi) + mm_nt(c3, lo)
     out[...] = acc
+    for copy in ahead:
+        copy.wait()
 
 
 def down_kernel(
     part, other, t0, t1, t2, near, basis, t_leaf, above,
-    out, near_v, t0_v, tl_v, out_v, in_sems, out_sems,
+    out, out_v, out_sems,
 ):
-    arrivals = copies(
-        [(t0, t0_v), (t_leaf, tl_v)] + [(near.at[k], near_v.at[k]) for k in range(4)], in_sems)
-    for copy in arrivals:
-        copy.start()
-
     def departure(step):
         cols = pl.ds(pl.multiple_of(step * 2048, 2048), 2048)
         return pltpu.make_async_copy(out_v.at[step], out.at[:, cols], out_sems.at[step])
@@ -268,18 +279,15 @@
     t3 = part[...] + other[...]
     g2 = t2[...] + fold(mm_nt(stacked(t3), above[4]))
     g1 = t1[...] + fold(mm_nt(stacked(g2), above[:4].reshape(512, 128)))
-    for copy in arrivals[:2]:
-        copy.wait()
     g0 = []
     for step in range(4):
         here = stacked(g1[:, 128 * step:128 * (step + 1)])
-        g0.append((t0_v[step] + fold(mm_nt(here, tl_v[4 * step:4 * step + 4].reshape(512, 128)))).astype(BF))
-    for step in range(4):
-        arrivals[2 + step].wait()
+        g0.append((t0[step] + fold(mm_nt(here, t_leaf[4 * step:4 * step + 4].reshape(512, 128)))).astype(BF))
+    for step in range(4):
         for q in range(4):
             cols = slice(512 * q, 512 * (q + 1))
-            far = mm_nt(g0[step][:, 128 * q:128 * (q + 1)], basis[4 * step + q])
-            out_v[step, :, cols] = (near_v[step, :, cols].astype(F32) + far).astype(BF)
+            far = mm(g0[step][:, 128 * q:128 * (q + 1)], basis[4 * step + q])
+            out_v[step, :, cols] = (near[step, :, cols].astype(F32) + far).astype(BF)
         departure(step).start()
     for step in range(4):
         departure(step).wait()
@@ -322,14 +330,14 @@
             rhs_block, points, basis, skeleton_leaf, skeleton_lower, skeleton_upper,
             skeleton_top, *transfers),
         [
-            ((32, 128), i32, vmem), ((4, 32, 512), F32, vmem), ((4, 64, 512), BF, vmem),
+            ((32, 128), i32, vmem), ((4, 32, 512), F32, hbm), ((4, 64, 512), BF, hbm),
             ((32, 512), F32, vmem), ((64, 512), BF, vmem), ((4, 160, 128), BF, vmem),
         ],
         [
             vmem((4, 32, 2048), BF), vmem((4, 32, 2048), F32), vmem((4, 4, 512, 128), BF),
             vmem((4, 4, 128, 128), BF), vmem((4, 128, 128), BF), vmem((1, 128, 128), BF),
             vmem((16, 128), i32), vmem((4, 128), i32), vmem((1, 128), i32),
-            dma((6,)), dma((16,)),
+            vmem((4, 32, 512), F32), vmem((4, 64, 512), BF), dma((6,)), dma((16,)), dma((8,)),
         ],
         pl.CostEstimate(flops=10**9, bytes_accessed=5 * 10**6, transcendentals=0),
     )
@@ -352,34 +360,36 @@
 
     near, t0, t1, t2, gens, above = call(
         near_kernel, "near",
-        outside(rhs_block, points, basis, transfer_lower, transfer_upper)
-        + inside(c0, s0, c1, s1, got1, place3),
-        [
-            ((4, 32, 2048), BF, hbm), ((4, 32, 512), F32, hbm),
+        outside(rhs_block, points, basis, transfer_lower, transfer_upper, c0, s0)
+        + inside(c1, s1, got1, place3),
+        [
+            ((4, 32, 2048), BF, hbm), ((4, 32, 512), F32, vmem),
             ((32, 512), F32, vmem), ((32, 128), F32, vmem),
-            ((16, 512, 128), BF, vmem), ((5, 128, 128), BF, vmem),
-        ],
-        [
-            vmem((4, 32, 2048), BF), vmem((4, 32, 2048), F32), vmem((4, 32, 2048), BF),
-            vmem((4, 32, 512), F32), dma((3,)), dma((8,)), dma((8,)),
+            ((16, 128, 512), BF, vmem), ((5, 128, 128), BF, vmem),
+        ],
+        [
+            vmem((4, 32, 2048), BF), vmem((4, 32, 2048), F32), vmem((4, 4, 512, 128), BF),
+            vmem((4, 32, 512), F32), vmem((4, 64, 512), BF), vmem((4, 32, 2048), BF),
+            dma((2,)), dma((20,)), dma((4,)),
         ],
         pl.CostEstimate(flops=6 * 10**9, bytes_accessed=3 * 10**6, transcendentals=5 * 10**6),
     )
 
-    part, = call(
-        top_kernel, "top", inside(got2, place3, t2), [((32, 128), F32, vmem)])
+    part, near, t_leaf = call(
+        top_kernel, "top", inside(got2, place3) + outside(near, transfer_leaf),
+        [((32, 128), F32, vmem), ((4, 32, 2048), BF, vmem), ((16, 128, 128), BF, vmem)],
+        [dma((2,))],
+    )
 
     partner = [(i, i ^ 1) for i in range(4 * nodes)]
     other = lax.ppermute(part, "leaf", partner)
 
     product, = call(
         down_kernel, "downward",
-        inside(part, other) + outside(t0) + inside(t1, t2) + outside(near)
-        + inside(gens) + outside(transfer_leaf) + inside(above),
+        inside(part, other, t0, t1, t2, near, gens, t_leaf, above),
         [((32, 8192), BF, hbm)],
         [
-            vmem((4, 32, 2048), BF), vmem((4, 32, 512), F32), vmem((16, 128, 128), BF),
-            vmem((4, 32, 2048), BF), dma((6,)), dma((4,)),
+            vmem((4, 32, 2048), BF), dma((4,)),
         ],
         pl.CostEstimate(flops=2 * 10**9, bytes_accessed=5 * 10**6, transcendentals=10**6),
     )

time: 53.8 us -> 51.1 us (0.950)
  the two profiles are of different devices: /device:TPU:65 before, /device:TPU:67 now
where the time goes in v3:
time: 51.1 us; the launch traced here: 50.8 us
  starting transfers between devices  20.6 us (40%)
  Pallas kernels  16.6 us (32%)
  waiting for transfers between devices  7.03 us (14%)
  blocking collectives  6.52 us (13%)
    pallas_call x5, Pallas kernels, call(): pl.pallas_call(kernel, in_specs=[spec(space) for _, space in ins], out_sp...  16.6 us
    all_to_all x1, starting transfers between devices, per_device(): lax.all_to_all(msg2, 'leaf', 0, 0, axis_index_groups=across, tiled=True)  15.9 us
    all_to_all x1, blocking collectives, per_device(): lax.all_to_all(msg1, 'leaf', 0, 0, axis_index_groups=siblings, tiled=True)  6.52 us
    all_to_all x1, waiting for transfers between devices, per_device(): lax.all_to_all(msg2, 'leaf', 0, 0, axis_index_groups=across, tiled=True)  6.21 us
    ppermute x1, starting transfers between devices, per_device(): other = lax.ppermute(part, 'leaf', partner)  4.77 us
  transfers between devices with their start and end apart: 2, of which 2 were waited for; matrix products, arithmetic and copies ran while one was open for 0% of the time, Pallas kernels for 18%

profile of v3, /device:TPU:67, one launch (start us, length us, event | category | flops | bytes accessed | tf_op | source)
XLA Modules:
  0.0 50.8 jit_solution(14563299992963217005)
XLA Ops:
  0.0 3.8 %upward.1 = (s32[32,128]{1,0:T(8,128)S(1)}, f32[4,32,512]{2,1,0:T(8,128)}, bf16[4,64,512]{2,1,0:T(8,128)(2,1)}, f32[32,512]{1,0:T(8,128)S(1)}, bf16[64,512]{1,0:...) custom-call(bf16[32,8192]{1,0:T(8,128)(2,1)} %rhs.3, f32[32,8192]{1,0:T(8,128)} %pts.3, bf16[16,512,128]{2,1,0:T(8,128)(2,1)} %basis.3, ...), custom_call_target="tpu_custom_call" | custom-call | flops 1000000000 | bytes 5000000 | tf_op jit(solution)/shard_map/upward/pallas_call | solution.py:298
  3.8 6.5 %all_to_all.10.got = bf16[4,160,128]{2,1,0:T(8,128)(2,1)S(1)} all-to-all(bf16[4,160,128]{2,1,0:T(8,128)(2,1)S(1)} %get-tuple-element.22), channel_id=1, replica_groups={{0,4,8,12},{16,20,24,28},{32,36,40,44},{48,52,56,60},{64,68,72,76},{80,..., dimensions={0} | all-to-all | bytes 327680 | tf_op jit(solution)/shard_map/all_to_all | solution.py:352
  10.3 1.0 %middle.1 = (bf16[32,48,128]{2,1,0:T(8,128)(2,1)}, bf16[64,128]{1,0:T(8,128)(2,1)S(1)}) custom-call(bf16[4,160,128]{2,1,0:T(8,128)(2,1)S(1)} %all_to_all.10.got, s32[32,128]{1,0:T(8,128)S(1)} %get-tuple-element.23.idx_top), custom_call_target="tpu_custom_call" | custom-call | tf_op jit(solution)/shard_map/middle/pallas_call | solution.py:298
  11.3 15.9 %all-to-all-start.1 = ((bf16[32,48,128]{2,1,0:T(8,128)(2,1)}), bf16[32,48,128]{2,1,0:T(8,128)(2,1)S(1)}, u32[]{:S(2)}, u32[]{:S(2)}) async-start(bf16[32,48,128]{2,1,0:T(8,128)(2,1)} %get-tuple-element.24), calls=%async_computation.1 | async-start | bytes 786432 | tf_op jit(solution)/shard_map/all_to_all | solution.py:359
  27.2 9.0 %near.1 = (bf16[4,32,2048]{2,1,0:T(8,128)(2,1)}, f32[4,32,512]{2,1,0:T(8,128)S(1)}, f32[32,512]{1,0:T(8,128)S(1)}, f32[32,128]{1,0:T(8,128)S(1)}, bf16[16,128,51...) custom-call(bf16[32,8192]{1,0:T(8,128)(2,1)} %rhs.3, f32[32,8192]{1,0:T(8,128)} %pts.3, ...), custom_call_target="tpu_custom_call" | custom-call | flops 6000000000 | bytes 3000000 | tf_op jit(solution)/shard_map/near/pallas_call | solution.py:298
  36.2 6.2 %all-to-all-done.1.got = bf16[32,48,128]{2,1,0:T(8,128)(2,1)S(1)} async-done(((bf16[32,48,128]{2,1,0:T(8,128)(2,1)}), bf16[32,48,128]{2,1,0:T(8,128)(2,1)S(1)}, u32[]{:S(2)}, u32[]{:S(2)}) %all-to-all-start.1) | async-done | bytes 393248 | tf_op jit(solution)/shard_map/all_to_all | solution.py:359
  42.5 1.2 %top.1 = (f32[32,128]{1,0:T(8,128)S(1)}, bf16[4,32,2048]{2,1,0:T(8,128)(2,1)S(1)}, bf16[16,128,128]{2,1,0:T(8,128)(2,1)S(1)}) custom-call(bf16[32,48,128]{2,1,0:T(8,128)(2,1)S(1)} %all-to-all-done.1.got, bf16[64,128]{1,0:T(8,128)(2,1)S(1)} %get-tuple-element.25.place3, bf16[4,32,2048]{2,1,0:T(8,128)(2,1)} %get-tuple-element.30.near, bf16[16,128,128]{2,1,0:T(8,128)(2,1)} %t_leaf.3), custom_call_target="tpu_custom_call" | custom-call | tf_op jit(solution)/shard_map/top/pallas_call | solution.py:298
  43.7 4.8 %collective-permute-start = (f32[32,128]{1,0:T(8,128)S(1)}, f32[32,128]{1,0:T(8,128)S(1)}, u32[]{:S(2)}, u32[]{:S(2)}) collective-permute-start(f32[32,128]{1,0:T(8,128)S(1)} %get-tuple-element.31.part), channel_id=1, source_target_pairs={{0,4},{4,0},{8,12},{12,8},{16,20},{20,16},{24,28},{28,24},{32,36},... | collective-permute-start | bytes 49160 | tf_op jit(solution)/shard_map/ppermute | solution.py:385
  48.5 0.8 %collective-permute-done.other = f32[32,128]{1,0:T(8,128)S(1)} collective-permute-done((f32[32,128]{1,0:T(8,128)S(1)}, f32[32,128]{1,0:T(8,128)S(1)}, u32[]{:S(2)}, u32[]{:S(2)}) %collective-permute-start) | collective-permute-done | bytes 16416 | tf_op jit(solution)/shard_map/ppermute | solution.py:385
  49.3 1.5 %downward.1 = bf16[32,8192]{1,0:T(8,128)(2,1)} custom-call(f32[32,128]{1,0:T(8,128)S(1)} %get-tuple-element.31.part, f32[32,128]{1,0:T(8,128)S(1)} %collective-permute-done.other, f32[4,32,512]{2,1,0:T(8,128)S(1)} %get-tuple-element.32.t0, f32[32,512]{1,0:T(8,128)S(1)} %get-tuple-element.33.t1, f32[32,128]{1,0:T(8,128)S(1)} %get-tuple-element.34.t2, ...), custom_call_target="tpu_custom_call" | custom-call | flops 2000000000 | bytes 5000000 | tf_op jit(solution)/shard_map/downward/pallas_call | solution.py:298
Async XLA Ops:
  11.3 31.1 %all-to-all-start.1 = ((bf16[32,48,128]{2,1,0:T(8,128)(2,1)}), bf16[32,48,128]{2,1,0:T(8,128)(2,1)S(1)}, u32[]{:S(2)}, u32[]{:S(2)}) async-start(bf16[32,48,128]{2,1,0:T(8,128)(2,1)} %get-tuple-element.24), calls=%async_computation.1 | async-start | bytes 786432 | tf_op jit(solution)/shard_map/all_to_all | solution.py:359
  43.7 5.6 %collective-permute-start = (f32[32,128]{1,0:T(8,128)S(1)}, f32[32,128]{1,0:T(8,128)S(1)}, u32[]{:S(2)}, u32[]{:S(2)}) collective-permute-start(f32[32,128]{1,0:T(8,128)S(1)} %get-tuple-element.31.part), channel_id=1, source_target_pairs={{0,4},{4,0},{8,12},{12,8},{16,20},{20,16},{24,28},{28,24},{32,36},... | collective-permute-start | bytes 49160 | tf_op jit(solution)/shard_map/ppermute | solution.py:385

commit v4 on v3

--- a/solution.py
+++ b/solution.py
@@ -8,6 +8,9 @@
 RIDGE = 1.0
 SCALE = (2.0 * 1.4426950408889634) ** 0.5
 BF = jnp.bfloat16
+PLACE_STEPS = 12800.0
+LOG_STEPS = 128.0
+LOG_ZERO = 127.0
 F32 = jnp.float32
 VMEM_LIMIT = 32 * 1024 * 1024
 
@@ -147,15 +150,17 @@
     s2 = jnp.concatenate([got[k, 96:160, :] for k in range(4)], axis=1)
     s3 = mm(s2, chosen(idx_top[pl.ds(position // 4, 1), :], 512))
     place_out[...] = s3.astype(BF)
-    rows = jnp.concatenate([c3, s3], axis=0)
-    moved = pltpu.roll(rows, 64, 1)
-    low = lax.broadcasted_iota(jnp.int32, (48, 128), 1) < 64
+    place = jnp.floor((s3[:32] + s3[32:]) * PLACE_STEPS + 0.5)
+    level = LOG_STEPS * (jnp.log2(jnp.maximum(jnp.abs(c3), 1e-38)) + LOG_ZERO)
+    level = jnp.clip(jnp.floor(level + 0.5), 0.0, 32767.0)
+    coeff = jnp.where(c3 < 0.0, -level, level)
+    low = lax.broadcasted_iota(jnp.int32, (32, 128), 1) < 64
     first = position % 2 == 0
     msg = jnp.where(
         low,
-        jnp.where(first, rows[:48], moved[:48]),
-        jnp.where(first, moved[48:], rows[48:]),
-    ).astype(BF)
+        jnp.where(first, coeff, pltpu.roll(coeff, 64, 1)),
+        jnp.where(first, pltpu.roll(place, 64, 1), place),
+    ).astype(jnp.int32).astype(jnp.int16)
     for k in range(32):
         msg_out[k] = msg
 
@@ -247,22 +252,25 @@
         copy.start()
     node = lax.axis_index("leaf") // 4
     target, _ = operands(place3[:32, :], place3[32:, :])
-    low = lax.broadcasted_iota(jnp.int32, (48, 128), 1) < 64
+    low = lax.broadcasted_iota(jnp.int32, (32, 128), 1) < 64
     column = lax.broadcasted_iota(jnp.int32, (32, 512), 1)
     acc = jnp.zeros((32, 128), F32)
     for first in range(0, 32, 8):
-        parts = []
+        coeffs, places = [], []
         for k in range(first, first + 8, 2):
-            even, odd = got[k].astype(F32), got[k + 1].astype(F32)
-            parts.append(jnp.concatenate([
-                jnp.where(low, even, pltpu.roll(odd, 64, 1)),
-                jnp.where(low, pltpu.roll(even, 64, 1), odd),
-            ], axis=0))
-        rows = jnp.concatenate(parts, axis=1)
-        c3 = jnp.where(column // 64 == node - first, 0.0, rows[:32]).astype(BF)
-        _, source = operands(rows[32:64].astype(BF), rows[64:].astype(BF))
+            even = got[k].astype(jnp.int32).astype(F32)
+            odd = got[k + 1].astype(jnp.int32).astype(F32)
+            coeffs.append(jnp.where(low, even, pltpu.roll(odd, 64, 1)))
+            places.append(jnp.where(low, pltpu.roll(even, 64, 1), odd))
+        level = jnp.concatenate(coeffs, axis=1)
+        size = jnp.exp2(jnp.abs(level) * (1.0 / LOG_STEPS) - LOG_ZERO)
+        c3 = jnp.where(level < 0.0, -size, size)
+        c3 = jnp.where((level == 0.0) | (column // 64 == node - first), 0.0, c3)
+        place = jnp.concatenate(places, axis=1) * (1.0 / PLACE_STEPS)
+        _, source = operands(*halves(place))
         hi, lo = halves(jnp.exp2(mm_tn(target, source)))
-        acc = acc + mm_nt(c3, hi) + mm_nt(c3, lo)
+        chl = stacked(c3)
+        acc = acc + fold(mm_nt(chl, hi)) + mm_nt(chl[:32], lo)
     out[...] = acc
     for copy in ahead:
         copy.wait()
@@ -353,7 +361,7 @@
 
     msg2, place3 = call(
         mid_kernel, "middle", inside(got1, top_index),
-        [((32, 48, 128), BF, vmem), ((64, 128), BF, vmem)],
+        [((32, 32, 128), jnp.int16, vmem), ((64, 128), BF, vmem)],
     )
 
     got2 = lax.all_to_all(msg2, "leaf", 0, 0, axis_index_groups=across, tiled=True)

time: 51.1 us -> 48.4 us (0.947)
  waiting for transfers between devices: 7.03 us -> 5.04 us
  starting transfers between devices: 20.6 us -> 20 us
    all_to_all x1, waiting for transfers between devices: 6.21 us -> 4.22 us  [per_device(): lax.all_to_all(msg2, 'leaf', 0, 0, axis_index_groups=across, tiled=True)]
    ppermute x1, starting transfers between devices: 4.77 us -> 4.1 us  [per_device(): other = lax.ppermute(part, 'leaf', partner)]
  transfers between devices with their start and end apart: 2 -> 2, of which waited for: 2 -> 2; matrix products, arithmetic and copies ran while one was open for 0% -> 0% of each run, Pallas kernels for 18% -> 19%
where the time goes in v4:
time: 48.4 us; the launch traced here: 48.1 us
  starting transfers between devices  20 us (41%)
  Pallas kernels  16.6 us (34%)
  blocking collectives  6.52 us (13%)
  waiting for transfers between devices  5.04 us (10%)
    pallas_call x5, Pallas kernels, call(): pl.pallas_call(kernel, in_specs=[spec(space) for _, space in ins], out_sp...  16.6 us
    all_to_all x1, starting transfers between devices, per_device(): lax.all_to_all(msg2, 'leaf', 0, 0, axis_index_groups=across, tiled=True)  15.9 us
    all_to_all x1, blocking collectives, per_device(): lax.all_to_all(msg1, 'leaf', 0, 0, axis_index_groups=siblings, tiled=True)  6.52 us
    all_to_all x1, waiting for transfers between devices, per_device(): lax.all_to_all(msg2, 'leaf', 0, 0, axis_index_groups=across, tiled=True)  4.22 us
    ppermute x1, starting transfers between devices, per_device(): other = lax.ppermute(part, 'leaf', partner)  4.1 us
  transfers between devices with their start and end apart: 2, of which 2 were waited for; matrix products, arithmetic and copies ran while one was open for 0% of the time, Pallas kernels for 19%

profile of v4, /device:TPU:67, one launch (start us, length us, event | category | flops | bytes accessed | tf_op | source)
XLA Modules:
  0.0 48.1 jit_solution(18076366984097647525)
XLA Ops:
  0.0 3.8 %upward.1 = (s32[32,128]{1,0:T(8,128)S(1)}, f32[4,32,512]{2,1,0:T(8,128)}, bf16[4,64,512]{2,1,0:T(8,128)(2,1)}, f32[32,512]{1,0:T(8,128)S(1)}, bf16[64,512]{1,0:...) custom-call(bf16[32,8192]{1,0:T(8,128)(2,1)} %rhs.3, f32[32,8192]{1,0:T(8,128)} %pts.3, bf16[16,512,128]{2,1,0:T(8,128)(2,1)} %basis.3, ...), custom_call_target="tpu_custom_call" | custom-call | flops 1000000000 | bytes 5000000 | tf_op jit(solution)/shard_map/upward/pallas_call | solution.py:306
  3.8 6.5 %all_to_all.10.got = bf16[4,160,128]{2,1,0:T(8,128)(2,1)S(1)} all-to-all(bf16[4,160,128]{2,1,0:T(8,128)(2,1)S(1)} %get-tuple-element.22), channel_id=1, replica_groups={{0,4,8,12},{16,20,24,28},{32,36,40,44},{48,52,56,60},{64,68,72,76},{80,..., dimensions={0} | all-to-all | bytes 327680 | tf_op jit(solution)/shard_map/all_to_all | solution.py:360
  10.3 1.0 %middle.1 = (s16[32,32,128]{2,1,0:T(8,128)(2,1)}, bf16[64,128]{1,0:T(8,128)(2,1)S(1)}) custom-call(bf16[4,160,128]{2,1,0:T(8,128)(2,1)S(1)} %all_to_all.10.got, s32[32,128]{1,0:T(8,128)S(1)} %get-tuple-element.23.idx_top), custom_call_target="tpu_custom_call" | custom-call | tf_op jit(solution)/shard_map/middle/pallas_call | solution.py:306
  11.3 15.9 %all-to-all-start.1 = ((s16[32,32,128]{2,1,0:T(8,128)(2,1)}), s16[32,32,128]{2,1,0:T(8,128)(2,1)S(1)}, u32[]{:S(2)}, u32[]{:S(2)}) async-start(s16[32,32,128]{2,1,0:T(8,128)(2,1)} %get-tuple-element.24), calls=%async_computation.1 | async-start | bytes 524288 | tf_op jit(solution)/shard_map/all_to_all | solution.py:367
  27.2 9.0 %near.1 = (bf16[4,32,2048]{2,1,0:T(8,128)(2,1)}, f32[4,32,512]{2,1,0:T(8,128)S(1)}, f32[32,512]{1,0:T(8,128)S(1)}, f32[32,128]{1,0:T(8,128)S(1)}, bf16[16,128,51...) custom-call(bf16[32,8192]{1,0:T(8,128)(2,1)} %rhs.3, f32[32,8192]{1,0:T(8,128)} %pts.3, ...), custom_call_target="tpu_custom_call" | custom-call | flops 6000000000 | bytes 3000000 | tf_op jit(solution)/shard_map/near/pallas_call | solution.py:306
  36.2 4.2 %all-to-all-done.1.got = s16[32,32,128]{2,1,0:T(8,128)(2,1)S(1)} async-done(((s16[32,32,128]{2,1,0:T(8,128)(2,1)}), s16[32,32,128]{2,1,0:T(8,128)(2,1)S(1)}, u32[]{:S(2)}, u32[]{:S(2)}) %all-to-all-start.1) | async-done | bytes 262176 | tf_op jit(solution)/shard_map/all_to_all | solution.py:367
  40.4 1.2 %top.1 = (f32[32,128]{1,0:T(8,128)S(1)}, bf16[4,32,2048]{2,1,0:T(8,128)(2,1)S(1)}, bf16[16,128,128]{2,1,0:T(8,128)(2,1)S(1)}) custom-call(s16[32,32,128]{2,1,0:T(8,128)(2,1)S(1)} %all-to-all-done.1.got, bf16[64,128]{1,0:T(8,128)(2,1)S(1)} %get-tuple-element.25.place3, bf16[4,32,2048]{2,1,0:T(8,128)(2,1)} %get-tuple-element.30.near, bf16[16,128,128]{2,1,0:T(8,128)(2,1)} %t_leaf.3), custom_call_target="tpu_custom_call" | custom-call | tf_op jit(solution)/shard_map/top/pallas_call | solution.py:306
  41.7 4.1 %collective-permute-start = (f32[32,128]{1,0:T(8,128)S(1)}, f32[32,128]{1,0:T(8,128)S(1)}, u32[]{:S(2)}, u32[]{:S(2)}) collective-permute-start(f32[32,128]{1,0:T(8,128)S(1)} %get-tuple-element.31.part), channel_id=1, source_target_pairs={{0,4},{4,0},{8,12},{12,8},{16,20},{20,16},{24,28},{28,24},{32,36},... | collective-permute-start | bytes 49160 | tf_op jit(solution)/shard_map/ppermute | solution.py:393
  45.8 0.8 %collective-permute-done.other = f32[32,128]{1,0:T(8,128)S(1)} collective-permute-done((f32[32,128]{1,0:T(8,128)S(1)}, f32[32,128]{1,0:T(8,128)S(1)}, u32[]{:S(2)}, u32[]{:S(2)}) %collective-permute-start) | collective-permute-done | bytes 16416 | tf_op jit(solution)/shard_map/ppermute | solution.py:393
  46.6 1.6 %downward.1 = bf16[32,8192]{1,0:T(8,128)(2,1)} custom-call(f32[32,128]{1,0:T(8,128)S(1)} %get-tuple-element.31.part, f32[32,128]{1,0:T(8,128)S(1)} %collective-permute-done.other, f32[4,32,512]{2,1,0:T(8,128)S(1)} %get-tuple-element.32.t0, f32[32,512]{1,0:T(8,128)S(1)} %get-tuple-element.33.t1, f32[32,128]{1,0:T(8,128)S(1)} %get-tuple-element.34.t2, ...), custom_call_target="tpu_custom_call" | custom-call | flops 2000000000 | bytes 5000000 | tf_op jit(solution)/shard_map/downward/pallas_call | solution.py:306
Async XLA Ops:
  11.3 29.1 %all-to-all-start.1 = ((s16[32,32,128]{2,1,0:T(8,128)(2,1)}), s16[32,32,128]{2,1,0:T(8,128)(2,1)S(1)}, u32[]{:S(2)}, u32[]{:S(2)}) async-start(s16[32,32,128]{2,1,0:T(8,128)(2,1)} %get-tuple-element.24), calls=%async_computation.1 | async-start | bytes 524288 | tf_op jit(solution)/shard_map/all_to_all | solution.py:367
  41.7 4.9 %collective-permute-start = (f32[32,128]{1,0:T(8,128)S(1)}, f32[32,128]{1,0:T(8,128)S(1)}, u32[]{:S(2)}, u32[]{:S(2)}) collective-permute-start(f32[32,128]{1,0:T(8,128)S(1)} %get-tuple-element.31.part), channel_id=1, source_target_pairs={{0,4},{4,0},{8,12},{12,8},{16,20},{20,16},{24,28},{28,24},{32,36},... | collective-permute-start | bytes 49160 | tf_op jit(solution)/shard_map/ppermute | solution.py:393

commit v5 on v4

--- a/solution.py
+++ b/solution.py
@@ -134,9 +134,15 @@
     c2 = fold(mm(stacked(c1_v[...]), tlo_v[...].reshape(512, 128)))
     s2 = mm(s1_v[...], chosen(iu_v[...], 512)).astype(BF)
     raised = fold(mm(stacked(c2), tu_v[0]))
-    msg = jnp.concatenate([c2.astype(BF), stacked(raised), s2], axis=0)
+    hi = raised.astype(BF).astype(F32)
+    lo = raised - hi
+    low = lax.broadcasted_iota(jnp.int32, (32, 128), 1) < 64
+    halved = (
+        jnp.where(low, hi, pltpu.roll(lo, 64, 1)),
+        jnp.where(low, pltpu.roll(hi, 64, 1), lo),
+    )
     for k in range(4):
-        msg_v[k] = msg
+        msg_v[k] = jnp.concatenate([c2.astype(BF), halved[k % 2].astype(BF), s2], axis=0)
     for step in range(4):
         for copy in departures(step):
             copy.wait()
@@ -144,10 +150,11 @@
 
 def mid_kernel(got, idx_top, msg_out, place_out):
     position = lax.axis_index("leaf")
-    c3 = jnp.zeros((32, 128), F32)
+    raised = jnp.zeros((32, 128), F32)
     for k in range(4):
-        c3 = c3 + got[k, 32:64, :].astype(F32) + got[k, 64:96, :].astype(F32)
-    s2 = jnp.concatenate([got[k, 96:160, :] for k in range(4)], axis=1)
+        raised = raised + got[k, 32:64, :].astype(F32)
+    c3 = raised + pltpu.roll(raised, 64, 1)
+    s2 = jnp.concatenate([got[k, 64:128, :] for k in range(4)], axis=1)
     s3 = mm(s2, chosen(idx_top[pl.ds(position // 4, 1), :], 512))
     place_out[...] = s3.astype(BF)
     place = jnp.floor((s3[:32] + s3[32:]) * PLACE_STEPS + 0.5)
@@ -157,9 +164,7 @@
     low = lax.broadcasted_iota(jnp.int32, (32, 128), 1) < 64
     first = position % 2 == 0
     msg = jnp.where(
-        low,
-        jnp.where(first, coeff, pltpu.roll(coeff, 64, 1)),
-        jnp.where(first, pltpu.roll(place, 64, 1), place),
+        low, coeff, jnp.where(first, pltpu.roll(place, 64, 1), place)
     ).astype(jnp.int32).astype(jnp.int16)
     for k in range(32):
         msg_out[k] = msg
@@ -229,12 +234,12 @@
     lax.fori_loop(0, 4, chunk, 0)
     t1_out[...] = sibling_sum(c1[...], *operands(s1[:32, :], s1[32:, :]))
     mine = lax.axis_index("leaf") % 4
-    target, _ = operands(got[mine, 96:128, :], got[mine, 128:160, :])
+    target, _ = operands(got[mine, 64:96, :], got[mine, 96:128, :])
 
     def side(rows):
         return jnp.concatenate([got[k, rows, :] for k in range(4)], axis=1)
 
-    _, source = operands(side(slice(96, 128)), side(slice(128, 160)))
+    _, source = operands(side(slice(64, 96)), side(slice(96, 128)))
     hi, lo = halves(jnp.exp2(mm_tn(target, source)))
     c2 = jnp.concatenate(
         [jnp.where(mine == k, 0.0, got[k, 0:32, :].astype(F32)) for k in range(4)], axis=1
@@ -339,7 +344,7 @@
             skeleton_top, *transfers),
         [
             ((32, 128), i32, vmem), ((4, 32, 512), F32, hbm), ((4, 64, 512), BF, hbm),
-            ((32, 512), F32, vmem), ((64, 512), BF, vmem), ((4, 160, 128), BF, vmem),
+            ((32, 512), F32, vmem), ((64, 512), BF, vmem), ((4, 128, 128), BF, vmem),
         ],
         [
             vmem((4, 32, 2048), BF), vmem((4, 32, 2048), F32), vmem((4, 4, 512, 128), BF),

time: 48.4 us -> 47.9 us (0.990)
  waiting for transfers between devices: 5.04 us -> 4.04 us
  starting transfers between devices: 20 us -> 20.7 us
    ppermute x1, starting transfers between devices: 4.1 us -> 5.32 us  [per_device(): other = lax.ppermute(part, 'leaf', partner)]
    all_to_all x1, waiting for transfers between devices: 4.22 us -> 3.23 us  [per_device(): lax.all_to_all(msg2, 'leaf', 0, 0, axis_index_groups=across, tiled=True)]
where the time goes in v5:
time: 47.9 us; the launch traced here: 47.6 us
  starting transfers between devices  20.7 us (43%)
  Pallas kernels  16.6 us (35%)
  blocking collectives  6.16 us (13%)
  waiting for transfers between devices  4.04 us (8%)
    pallas_call x5, Pallas kernels, call(): pl.pallas_call(kernel, in_specs=[spec(space) for _, space in ins], out_sp...  16.6 us
    all_to_all x1, starting transfers between devices, per_device(): lax.all_to_all(msg2, 'leaf', 0, 0, axis_index_groups=across, tiled=True)  15.4 us
    all_to_all x1, blocking collectives, per_device(): lax.all_to_all(msg1, 'leaf', 0, 0, axis_index_groups=siblings, tiled=True)  6.16 us
    ppermute x1, starting transfers between devices, per_device(): other = lax.ppermute(part, 'leaf', partner)  5.32 us
    all_to_all x1, waiting for transfers between devices, per_device(): lax.all_to_all(msg2, 'leaf', 0, 0, axis_index_groups=across, tiled=True)  3.23 us
  transfers between devices with their start and end apart: 2, of which 2 were waited for; matrix products, arithmetic and copies ran while one was open for 0% of the time, Pallas kernels for 19%

profile of v5, /device:TPU:67, one launch (start us, length us, event | category | flops | bytes accessed | tf_op | source)
XLA Modules:
  0.0 47.6 jit_solution(13688732549306294829)
XLA Ops:
  0.0 3.8 %upward.1 = (s32[32,128]{1,0:T(8,128)S(1)}, f32[4,32,512]{2,1,0:T(8,128)}, bf16[4,64,512]{2,1,0:T(8,128)(2,1)}, f32[32,512]{1,0:T(8,128)S(1)}, bf16[64,512]{1,0:...) custom-call(bf16[32,8192]{1,0:T(8,128)(2,1)} %rhs.3, f32[32,8192]{1,0:T(8,128)} %pts.3, bf16[16,512,128]{2,1,0:T(8,128)(2,1)} %basis.3, ...), custom_call_target="tpu_custom_call" | custom-call | flops 1000000000 | bytes 5000000 | tf_op jit(solution)/shard_map/upward/pallas_call | solution.py:311
  3.9 6.2 %all_to_all.10.got = bf16[4,128,128]{2,1,0:T(8,128)(2,1)S(1)} all-to-all(bf16[4,128,128]{2,1,0:T(8,128)(2,1)S(1)} %get-tuple-element.22), channel_id=1, replica_groups={{0,4,8,12},{16,20,24,28},{32,36,40,44},{48,52,56,60},{64,68,72,76},{80,..., dimensions={0} | all-to-all | bytes 262144 | tf_op jit(solution)/shard_map/all_to_all | solution.py:365
  10.0 1.0 %middle.1 = (s16[32,32,128]{2,1,0:T(8,128)(2,1)}, bf16[64,128]{1,0:T(8,128)(2,1)S(1)}) custom-call(bf16[4,128,128]{2,1,0:T(8,128)(2,1)S(1)} %all_to_all.10.got, s32[32,128]{1,0:T(8,128)S(1)} %get-tuple-element.23.idx_top), custom_call_target="tpu_custom_call" | custom-call | tf_op jit(solution)/shard_map/middle/pallas_call | solution.py:311
  11.0 15.4 %all-to-all-start.1 = ((s16[32,32,128]{2,1,0:T(8,128)(2,1)}), s16[32,32,128]{2,1,0:T(8,128)(2,1)S(1)}, u32[]{:S(2)}, u32[]{:S(2)}) async-start(s16[32,32,128]{2,1,0:T(8,128)(2,1)} %get-tuple-element.24), calls=%async_computation.1 | async-start | bytes 524288 | tf_op jit(solution)/shard_map/all_to_all | solution.py:372
  26.4 9.0 %near.1 = (bf16[4,32,2048]{2,1,0:T(8,128)(2,1)}, f32[4,32,512]{2,1,0:T(8,128)S(1)}, f32[32,512]{1,0:T(8,128)S(1)}, f32[32,128]{1,0:T(8,128)S(1)}, bf16[16,128,51...) custom-call(bf16[32,8192]{1,0:T(8,128)(2,1)} %rhs.3, f32[32,8192]{1,0:T(8,128)} %pts.3, ...), custom_call_target="tpu_custom_call" | custom-call | flops 6000000000 | bytes 3000000 | tf_op jit(solution)/shard_map/near/pallas_call | solution.py:311
  35.4 3.2 %all-to-all-done.1.got = s16[32,32,128]{2,1,0:T(8,128)(2,1)S(1)} async-done(((s16[32,32,128]{2,1,0:T(8,128)(2,1)}), s16[32,32,128]{2,1,0:T(8,128)(2,1)S(1)}, u32[]{:S(2)}, u32[]{:S(2)}) %all-to-all-start.1) | async-done | bytes 262176 | tf_op jit(solution)/shard_map/all_to_all | solution.py:372
  38.7 1.2 %top.1 = (f32[32,128]{1,0:T(8,128)S(1)}, bf16[4,32,2048]{2,1,0:T(8,128)(2,1)S(1)}, bf16[16,128,128]{2,1,0:T(8,128)(2,1)S(1)}) custom-call(s16[32,32,128]{2,1,0:T(8,128)(2,1)S(1)} %all-to-all-done.1.got, bf16[64,128]{1,0:T(8,128)(2,1)S(1)} %get-tuple-element.25.place3, bf16[4,32,2048]{2,1,0:T(8,128)(2,1)} %get-tuple-element.30.near, bf16[16,128,128]{2,1,0:T(8,128)(2,1)} %t_leaf.3), custom_call_target="tpu_custom_call" | custom-call | tf_op jit(solution)/shard_map/top/pallas_call | solution.py:311
  39.9 5.3 %collective-permute-start = (f32[32,128]{1,0:T(8,128)S(1)}, f32[32,128]{1,0:T(8,128)S(1)}, u32[]{:S(2)}, u32[]{:S(2)}) collective-permute-start(f32[32,128]{1,0:T(8,128)S(1)} %get-tuple-element.31.part), channel_id=1, source_target_pairs={{0,4},{4,0},{8,12},{12,8},{16,20},{20,16},{24,28},{28,24},{32,36},... | collective-permute-start | bytes 49160 | tf_op jit(solution)/shard_map/ppermute | solution.py:398
  45.2 0.8 %collective-permute-done.other = f32[32,128]{1,0:T(8,128)S(1)} collective-permute-done((f32[32,128]{1,0:T(8,128)S(1)}, f32[32,128]{1,0:T(8,128)S(1)}, u32[]{:S(2)}, u32[]{:S(2)}) %collective-permute-start) | collective-permute-done | bytes 16416 | tf_op jit(solution)/shard_map/ppermute | solution.py:398
  46.1 1.5 %downward.1 = bf16[32,8192]{1,0:T(8,128)(2,1)} custom-call(f32[32,128]{1,0:T(8,128)S(1)} %get-tuple-element.31.part, f32[32,128]{1,0:T(8,128)S(1)} %collective-permute-done.other, f32[4,32,512]{2,1,0:T(8,128)S(1)} %get-tuple-element.32.t0, f32[32,512]{1,0:T(8,128)S(1)} %get-tuple-element.33.t1, f32[32,128]{1,0:T(8,128)S(1)} %get-tuple-element.34.t2, ...), custom_call_target="tpu_custom_call" | custom-call | flops 2000000000 | bytes 5000000 | tf_op jit(solution)/shard_map/downward/pallas_call | solution.py:311
Async XLA Ops:
  11.0 27.7 %all-to-all-start.1 = ((s16[32,32,128]{2,1,0:T(8,128)(2,1)}), s16[32,32,128]{2,1,0:T(8,128)(2,1)S(1)}, u32[]{:S(2)}, u32[]{:S(2)}) async-start(s16[32,32,128]{2,1,0:T(8,128)(2,1)} %get-tuple-element.24), calls=%async_computation.1 | async-start | bytes 524288 | tf_op jit(solution)/shard_map/all_to_all | solution.py:372
  39.9 6.1 %collective-permute-start = (f32[32,128]{1,0:T(8,128)S(1)}, f32[32,128]{1,0:T(8,128)S(1)}, u32[]{:S(2)}, u32[]{:S(2)}) collective-permute-start(f32[32,128]{1,0:T(8,128)S(1)} %get-tuple-element.31.part), channel_id=1, source_target_pairs={{0,4},{4,0},{8,12},{12,8},{16,20},{20,16},{24,28},{28,24},{32,36},... | collective-permute-start | bytes 49160 | tf_op jit(solution)/shard_map/ppermute | solution.py:398

commit v6 on v5

--- a/solution.py
+++ b/solution.py
@@ -186,12 +186,11 @@
 def near_kernel(
     rhs, pts, basis, t_lower, t_upper, c0, s0, c1, s1, got, place3,
     near_out, t0_out, t1_out, t2_out, basis_out, above_out,
-    rhs_v, pts_v, basis_v, c0_v, s0_v, near_v, sems, chunk_sems, out_sems,
+    rhs_v, pts_v, basis_v, above_v, c0_v, s0_v, near_v, sems, chunk_sems, out_sems,
 ):
     ahead = copies(
         [
-            (t_lower, above_out.at[pl.ds(0, 4)]),
-            (t_upper, above_out.at[pl.ds(4, 1)]),
+            (t_lower, above_v.at[pl.ds(0, 4)]), (t_upper, above_v.at[pl.ds(4, 1)]),
         ], sems)
 
     def arrivals(step):
@@ -247,6 +246,8 @@
     t2_out[...] = mm_nt(c2, hi) + mm_nt(c2, lo)
     for copy in ahead:
         copy.wait()
+    for k in range(5):
+        above_out[:, 128 * k:128 * (k + 1)] = above_v[k].T
     for step in range(4):
         departure(step).wait()
 
@@ -256,7 +257,7 @@
     for copy in ahead:
         copy.start()
     node = lax.axis_index("leaf") // 4
-    target, _ = operands(place3[:32, :], place3[32:, :])
+    _, target = operands(place3[:32, :], place3[32:, :])
     low = lax.broadcasted_iota(jnp.int32, (32, 128), 1) < 64
     column = lax.broadcasted_iota(jnp.int32, (32, 512), 1)
     acc = jnp.zeros((32, 128), F32)
@@ -272,10 +273,10 @@
         c3 = jnp.where(level < 0.0, -size, size)
         c3 = jnp.where((level == 0.0) | (column // 64 == node - first), 0.0, c3)
         place = jnp.concatenate(places, axis=1) * (1.0 / PLACE_STEPS)
-        _, source = operands(*halves(place))
-        hi, lo = halves(jnp.exp2(mm_tn(target, source)))
+        source, _ = operands(*halves(place))
+        hi, lo = halves(jnp.exp2(mm_tn(source, target)))
         chl = stacked(c3)
-        acc = acc + fold(mm_nt(chl, hi)) + mm_nt(chl[:32], lo)
+        acc = acc + fold(mm(chl, hi)) + mm(chl[:32], lo)
     out[...] = acc
     for copy in ahead:
         copy.wait()
@@ -290,8 +291,8 @@
         return pltpu.make_async_copy(out_v.at[step], out.at[:, cols], out_sems.at[step])
 
     t3 = part[...] + other[...]
-    g2 = t2[...] + fold(mm_nt(stacked(t3), above[4]))
-    g1 = t1[...] + fold(mm_nt(stacked(g2), above[:4].reshape(512, 128)))
+    g2 = t2[...] + fold(mm(stacked(t3), above[:, 512:]))
+    g1 = t1[...] + fold(mm(stacked(g2), above[:, :512]))
     g0 = []
     for step in range(4):
         here = stacked(g1[:, 128 * step:128 * (step + 1)])
@@ -378,10 +379,11 @@
         [
             ((4, 32, 2048), BF, hbm), ((4, 32, 512), F32, vmem),
             ((32, 512), F32, vmem), ((32, 128), F32, vmem),
-            ((16, 128, 512), BF, vmem), ((5, 128, 128), BF, vmem),
+            ((16, 128, 512), BF, vmem), ((128, 640), BF, vmem),
         ],
         [
             vmem((4, 32, 2048), BF), vmem((4, 32, 2048), F32), vmem((4, 4, 512, 128), BF),
+            vmem((5, 128, 128), BF),
             vmem((4, 32, 512), F32), vmem((4, 64, 512), BF), vmem((4, 32, 2048), BF),
             dma((2,)), dma((20,)), dma((4,)),
         ],

time: 47.9 us -> 47.8 us (level)
  no operation moved by 1% of the time
where the time goes in v6:
time: 47.8 us; the launch traced here: 47.6 us
  starting transfers between devices  20.7 us (43%)
  Pallas kernels  16.7 us (35%)
  blocking collectives  6.16 us (13%)
  waiting for transfers between devices  3.94 us (8%)
    pallas_call x5, Pallas kernels, call(): pl.pallas_call(kernel, in_specs=[spec(space) for _, space in ins], out_sp...  16.7 us
    all_to_all x1, starting transfers between devices, per_device(): lax.all_to_all(msg2, 'leaf', 0, 0, axis_index_groups=across, tiled=True)  15.4 us
    all_to_all x1, blocking collectives, per_device(): lax.all_to_all(msg1, 'leaf', 0, 0, axis_index_groups=siblings, tiled=True)  6.16 us
    ppermute x1, starting transfers between devices, per_device(): other = lax.ppermute(part, 'leaf', partner)  5.32 us
    all_to_all x1, waiting for transfers between devices, per_device(): lax.all_to_all(msg2, 'leaf', 0, 0, axis_index_groups=across, tiled=True)  3.12 us
  transfers between devices with their start and end apart: 2, of which 2 were waited for; matrix products, arithmetic and copies ran while one was open for 0% of the time, Pallas kernels for 19%

profile of v6, /device:TPU:67, one launch (start us, length us, event | category | flops | bytes accessed | tf_op | source)
XLA Modules:
  0.0 47.6 jit_solution(5633131007814256213)
XLA Ops:
  0.0 3.8 %upward.1 = (s32[32,128]{1,0:T(8,128)S(1)}, f32[4,32,512]{2,1,0:T(8,128)}, bf16[4,64,512]{2,1,0:T(8,128)(2,1)}, f32[32,512]{1,0:T(8,128)S(1)}, bf16[64,512]{1,0:...) custom-call(bf16[32,8192]{1,0:T(8,128)(2,1)} %rhs.3, f32[32,8192]{1,0:T(8,128)} %pts.3, bf16[16,512,128]{2,1,0:T(8,128)(2,1)} %basis.3, ...), custom_call_target="tpu_custom_call" | custom-call | flops 1000000000 | bytes 5000000 | tf_op jit(solution)/shard_map/upward/pallas_call | solution.py:312
  3.9 6.2 %all_to_all.10.got = bf16[4,128,128]{2,1,0:T(8,128)(2,1)S(1)} all-to-all(bf16[4,128,128]{2,1,0:T(8,128)(2,1)S(1)} %get-tuple-element.22), channel_id=1, replica_groups={{0,4,8,12},{16,20,24,28},{32,36,40,44},{48,52,56,60},{64,68,72,76},{80,..., dimensions={0} | all-to-all | bytes 262144 | tf_op jit(solution)/shard_map/all_to_all | solution.py:366
  10.0 1.0 %middle.1 = (s16[32,32,128]{2,1,0:T(8,128)(2,1)}, bf16[64,128]{1,0:T(8,128)(2,1)S(1)}) custom-call(bf16[4,128,128]{2,1,0:T(8,128)(2,1)S(1)} %all_to_all.10.got, s32[32,128]{1,0:T(8,128)S(1)} %get-tuple-element.23.idx_top), custom_call_target="tpu_custom_call" | custom-call | tf_op jit(solution)/shard_map/middle/pallas_call | solution.py:312
  11.0 15.4 %all-to-all-start.1 = ((s16[32,32,128]{2,1,0:T(8,128)(2,1)}), s16[32,32,128]{2,1,0:T(8,128)(2,1)S(1)}, u32[]{:S(2)}, u32[]{:S(2)}) async-start(s16[32,32,128]{2,1,0:T(8,128)(2,1)} %get-tuple-element.24), calls=%async_computation.1 | async-start | bytes 524288 | tf_op jit(solution)/shard_map/all_to_all | solution.py:373
  26.4 9.1 %near.1 = (bf16[4,32,2048]{2,1,0:T(8,128)(2,1)}, f32[4,32,512]{2,1,0:T(8,128)S(1)}, f32[32,512]{1,0:T(8,128)S(1)}, f32[32,128]{1,0:T(8,128)S(1)}, bf16[16,128,51...) custom-call(bf16[32,8192]{1,0:T(8,128)(2,1)} %rhs.3, f32[32,8192]{1,0:T(8,128)} %pts.3, bf16[16,512,128]{2,1,0:T(8,128)(2,1)} %basis.3, ...), custom_call_target="tpu_custom_call" | custom-call | flops 6000000000 | bytes 3000000 | tf_op jit(solution)/shard_map/near/pallas_call | solution.py:312
  35.5 3.1 %all-to-all-done.1.got = s16[32,32,128]{2,1,0:T(8,128)(2,1)S(1)} async-done(((s16[32,32,128]{2,1,0:T(8,128)(2,1)}), s16[32,32,128]{2,1,0:T(8,128)(2,1)S(1)}, u32[]{:S(2)}, u32[]{:S(2)}) %all-to-all-start.1) | async-done | bytes 262176 | tf_op jit(solution)/shard_map/all_to_all | solution.py:373
  38.7 1.2 %top.1 = (f32[32,128]{1,0:T(8,128)S(1)}, bf16[4,32,2048]{2,1,0:T(8,128)(2,1)S(1)}, bf16[16,128,128]{2,1,0:T(8,128)(2,1)S(1)}) custom-call(s16[32,32,128]{2,1,0:T(8,128)(2,1)S(1)} %all-to-all-done.1.got, bf16[64,128]{1,0:T(8,128)(2,1)S(1)} %get-tuple-element.25.place3, bf16[4,32,2048]{2,1,0:T(8,128)(2,1)} %get-tuple-element.30.near, bf16[16,128,128]{2,1,0:T(8,128)(2,1)} %t_leaf.3), custom_call_target="tpu_custom_call" | custom-call | tf_op jit(solution)/shard_map/top/pallas_call | solution.py:312
  39.9 5.3 %collective-permute-start = (f32[32,128]{1,0:T(8,128)S(1)}, f32[32,128]{1,0:T(8,128)S(1)}, u32[]{:S(2)}, u32[]{:S(2)}) collective-permute-start(f32[32,128]{1,0:T(8,128)S(1)} %get-tuple-element.31.part), channel_id=1, source_target_pairs={{0,4},{4,0},{8,12},{12,8},{16,20},{20,16},{24,28},{28,24},{32,36},... | collective-permute-start | bytes 49160 | tf_op jit(solution)/shard_map/ppermute | solution.py:400
  45.2 0.8 %collective-permute-done.other = f32[32,128]{1,0:T(8,128)S(1)} collective-permute-done((f32[32,128]{1,0:T(8,128)S(1)}, f32[32,128]{1,0:T(8,128)S(1)}, u32[]{:S(2)}, u32[]{:S(2)}) %collective-permute-start) | collective-permute-done | bytes 16416 | tf_op jit(solution)/shard_map/ppermute | solution.py:400
  46.1 1.5 %downward.1 = bf16[32,8192]{1,0:T(8,128)(2,1)} custom-call(f32[32,128]{1,0:T(8,128)S(1)} %get-tuple-element.31.part, f32[32,128]{1,0:T(8,128)S(1)} %collective-permute-done.other, f32[4,32,512]{2,1,0:T(8,128)S(1)} %get-tuple-element.32.t0, f32[32,512]{1,0:T(8,128)S(1)} %get-tuple-element.33.t1, f32[32,128]{1,0:T(8,128)S(1)} %get-tuple-element.34.t2, ...), custom_call_target="tpu_custom_call" | custom-call | flops 2000000000 | bytes 5000000 | tf_op jit(solution)/shard_map/downward/pallas_call | solution.py:312
Async XLA Ops:
  11.0 27.7 %all-to-all-start.1 = ((s16[32,32,128]{2,1,0:T(8,128)(2,1)}), s16[32,32,128]{2,1,0:T(8,128)(2,1)S(1)}, u32[]{:S(2)}, u32[]{:S(2)}) async-start(s16[32,32,128]{2,1,0:T(8,128)(2,1)} %get-tuple-element.24), calls=%async_computation.1 | async-start | bytes 524288 | tf_op jit(solution)/shard_map/all_to_all | solution.py:373
  39.9 6.1 %collective-permute-start = (f32[32,128]{1,0:T(8,128)S(1)}, f32[32,128]{1,0:T(8,128)S(1)}, u32[]{:S(2)}, u32[]{:S(2)}) collective-permute-start(f32[32,128]{1,0:T(8,128)S(1)} %get-tuple-element.31.part), channel_id=1, source_target_pairs={{0,4},{4,0},{8,12},{12,8},{16,20},{20,16},{24,28},{28,24},{32,36},... | collective-permute-start | bytes 49160 | tf_op jit(solution)/shard_map/ppermute | solution.py:400
